TPU v7x, 128 devices: a whole 4x4x4 slice. The times are simulated.
128 devices in a mesh: dev: 128 (over y, x, z, core).
Axes of the slice: x: 4, y: 4, z: 4, core: 2. Of those that a mesh axis runs over, the one named last changes fastest.
Arguments:
- params: float32 [59, 655360], P(None, 'dev'), as said below
- requests: int32 [128, 128, 40], P('dev'), may hold values from 0 to 5119, as said below
- tile_slots: int32 [2048, 512], P('dev'), may hold values from 0 to 5119, as said below
- tile_count: int32 [2048], P('dev'), may hold values from 128 to 512, as said below
- tile_place: int32 [2048], P('dev'), may hold values from 0 to 8159, as said below
- target: float32 [2048, 3, 256], P('dev'), may hold values from 0 to 1
Outputs:
- rendered: float32 [2048, 3, 256], P('dev')
- gradient: float32 [59, 655360], P(None, 'dev')
Inputs may be any that keep to these rules, and one draw needn't show every extreme that they name: requests[d, p, c] is a row (0 to 5119) of owner p's Gaussians; for each owner the lists of all devices name each of its rows exactly once. `tile_slots`: entries k < tile_count of a tile are rows of its device's received block, in front-to-back order; entries beyond hold 0; over the 16 tiles of a device every received row is listed exactly once. `tile_count`: the counts of one device's tiles sum to 5120. `tile_place`: all entries are distinct. `params`: row 2 lies between 2 and 8; row 6 between 0.5 and 1.5; rows 7 to 9 between -1 and 1.
All inputs are finite; a program needn't handle non-finite values.
Results may differ from a plain program's by a relative error of at most 0.0003.
Values sent between devices are 32-bit elements; how exact they have to be, the bound alone decides.
A program may use at most 128 MiB of HBM per device.

v0:
```python
import functools

import jax
import jax.numpy as jnp
from jax import lax
from jax.experimental import pallas as pl
from jax.experimental.pallas import tpu as pltpu
from jax.sharding import PartitionSpec as P

FOCAL = 1200.0
CENTER_X = 960.0
CENTER_Y = 540.0
DILATION = 0.3
BAND_ZERO = 0.28209479177387814
BAND_ONE = 0.4886025119029199
BAND_TWO = (
    1.0925484305920792,
    -1.0925484305920792,
    0.31539156525252005,
    -1.0925484305920792,
    0.5462742152960396,
)
BAND_THREE = (
    -0.5900435899266435,
    2.890611442640554,
    -0.4570457994644658,
    0.3731763325901154,
    -0.4570457994644658,
    1.445305721320277,
    -0.5900435899266435,
)
LOG2_E = 1.4426950408889634

DEVICES = 128
OWNED = 5120
CAP = 40
PARAMS = 59
BLOCKS = OWNED // 128
TILES = 16
SLOTS = 512
SEG = 46
SEG_PAD = 48
SEGS = 12
GROUP = 8
PASSES = 32 // GROUP
F32 = jnp.float32
I32 = jnp.int32
VMEM_LIMIT = 48 * 1024 * 1024


def project(rows):
    x, y, z = rows[0], rows[1], rows[2]
    scales = [jnp.exp(rows[3 + k]) for k in range(3)]
    norm = jnp.sqrt(rows[6] * rows[6] + rows[7] * rows[7] + rows[8] * rows[8] + rows[9] * rows[9])
    qw, qx, qy, qz = (rows[6 + k] / norm for k in range(4))
    rotation = [
        [1.0 - 2.0 * (qy * qy + qz * qz), 2.0 * (qx * qy - qw * qz), 2.0 * (qx * qz + qw * qy)],
        [2.0 * (qx * qy + qw * qz), 1.0 - 2.0 * (qx * qx + qz * qz), 2.0 * (qy * qz - qw * qx)],
        [2.0 * (qx * qz - qw * qy), 2.0 * (qy * qz + qw * qx), 1.0 - 2.0 * (qx * qx + qy * qy)],
    ]
    spread = [[rotation[i][k] * scales[k] for k in range(3)] for i in range(3)]
    inverse_z = 1.0 / z
    diag = FOCAL * inverse_z
    jac_xz = -FOCAL * x * inverse_z * inverse_z
    jac_yz = -FOCAL * y * inverse_z * inverse_z
    across = [diag * spread[0][k] + jac_xz * spread[2][k] for k in range(3)]
    upward = [diag * spread[1][k] + jac_yz * spread[2][k] for k in range(3)]
    cov_xx = across[0] * across[0] + across[1] * across[1] + across[2] * across[2] + DILATION
    cov_xy = across[0] * upward[0] + across[1] * upward[1] + across[2] * upward[2]
    cov_yy = upward[0] * upward[0] + upward[1] * upward[1] + upward[2] * upward[2] + DILATION
    determinant = cov_xx * cov_yy - cov_xy * cov_xy
    distance = jnp.sqrt(x * x + y * y + z * z)
    fx, fy, fz = x / distance, y / distance, z / distance
    xx, yy, zz = fx * fx, fy * fy, fz * fz
    basis = [
        None,
        -BAND_ONE * fy,
        BAND_ONE * fz,
        -BAND_ONE * fx,
        BAND_TWO[0] * fx * fy,
        BAND_TWO[1] * fy * fz,
        BAND_TWO[2] * (2.0 * zz - xx - yy),
        BAND_TWO[3] * fx * fz,
        BAND_TWO[4] * (xx - yy),
        BAND_THREE[0] * fy * (3.0 * xx - yy),
        BAND_THREE[1] * fx * fy * fz,
        BAND_THREE[2] * fy * (4.0 * zz - xx - yy),
        BAND_THREE[3] * fz * (2.0 * zz - 3.0 * xx - 3.0 * yy),
        BAND_THREE[4] * fx * (4.0 * zz - xx - yy),
        BAND_THREE[5] * fz * (xx - yy),
        BAND_THREE[6] * fx * (xx - 3.0 * yy),
    ]
    colours = []
    for channel in range(3):
        total = BAND_ZERO * rows[11 + channel]
        for k in range(1, 16):
            total = total + basis[k] * rows[11 + 3 * k + channel]
        colours.append(jnp.maximum(total + 0.5, 0.0))
    return [
        FOCAL * x * inverse_z + CENTER_X,
        FOCAL * y * inverse_z + CENTER_Y,
        cov_yy / determinant,
        -cov_xy / determinant,
        cov_xx / determinant,
        1.0 / (1.0 + jnp.exp(-rows[10])),
        *colours,
    ]


def load_rows(params_ref, group):
    columns = pl.ds(pl.multiple_of(group * 1024, 1024), 1024)
    return [params_ref[row : row + 1, columns].reshape(8, 128) for row in range(PARAMS)]


def project_kernel(params_ref, screen_ref, ninth_ref):
    def one_group(group, carry):
        screen = project(load_rows(params_ref, group))
        for row in range(8):
            screen_ref[pl.ds(pl.multiple_of(group * 8, 8), 8), row, :] = screen[row]
        ninth_ref[group] = screen[8]
        return carry

    lax.fori_loop(0, OWNED // 1024, one_group, 0)


def gather(source_ref, ninth_ref, block_ref, lane_ref, out_ref, out_ninth_ref, targets, sources):
    sublane = lax.broadcasted_iota(I32, (8, 128), 0)

    def one_row(row, carry):
        lane = jnp.broadcast_to(lane_ref[pl.ds(row, 1), :], (8, 128))
        block = jnp.broadcast_to(block_ref[pl.ds(row, 1), :], (8, 128))
        total = jnp.zeros((8, 128), F32)
        for source in range(sources):
            picked = jnp.take_along_axis(source_ref[source], lane, axis=1)
            total = jnp.where(block == source, picked, total)
        out_ref[row] = total
        place = block - sublane
        total = jnp.zeros((8, 128), F32)
        for source in range((sources + 7) // 8):
            picked = jnp.take_along_axis(ninth_ref[source], lane, axis=1)
            total = jnp.where(place == 8 * source, picked, total)
        out_ninth_ref[pl.ds(row, 1), :] = jnp.sum(total, axis=0, keepdims=True)
        return carry

    lax.fori_loop(0, targets, one_row, 0)


def invert(block_ref, lane_ref, left_ref, right_ref, row_ref, col_ref, rows, blocks):
    iota_lane = lax.broadcasted_iota(I32, (1, 128), 1).astype(F32)
    iota_block = lax.broadcasted_iota(I32, (blocks, 128), 0)
    iota_sub = lax.broadcasted_iota(I32, (128, 128), 0)

    def one_row(row, carry):
        columns = pl.ds(pl.multiple_of(row * 128, 128), 128)
        here = iota_block == block_ref[pl.ds(row, 1), :]
        value = jnp.full((1, 128), 0.0, F32) + row.astype(F32)
        left_ref[0:blocks, columns] = jnp.where(here, value, 0.0).astype(jnp.bfloat16)
        left_ref[blocks : 2 * blocks, columns] = jnp.where(here, iota_lane, 0.0).astype(
            jnp.bfloat16
        )
        right_ref[:, columns] = jnp.where(
            iota_sub == lane_ref[pl.ds(row, 1), :], 1.0, 0.0
        ).astype(jnp.bfloat16)
        return carry

    lax.fori_loop(0, rows, one_row, 0)
    found = lax.dot_general(
        left_ref[...], right_ref[...], (((1,), (1,)), ((), ())), preferred_element_type=F32
    )
    row_ref[...] = (found[0:blocks] + 0.5).astype(I32)
    col_ref[...] = (found[blocks : 2 * blocks] + 0.5).astype(I32)


def pack_messages(rows_ref, ninth_ref, out_ref):
    flat = rows_ref[...].reshape(CAP * 8, 128)
    out_ref[:, 0, :] = flat[0:128].T
    out_ref[:, 1, :] = flat[128:256].T
    last = jnp.concatenate(
        [flat[256:320], ninth_ref[...], jnp.zeros((128 - 64 - CAP, 128), F32)], axis=0
    )
    out_ref[:, 2, :] = last.T
    out_ref[:, 3, :] = jnp.zeros((128, 128), F32)


def unpack_messages(message_ref, rows_ref, ninth_ref):
    rows_ref[0:16] = message_ref[:, 0, :].T.reshape(16, 8, 128)
    rows_ref[16:32] = message_ref[:, 1, :].T.reshape(16, 8, 128)
    last = message_ref[:, 2, :].T
    rows_ref[32:40] = last[0:64].reshape(8, 8, 128)
    ninth_ref[...] = last[64 : 64 + CAP].reshape(CAP // 8, 8, 128)


def wanted_tables(wanted_ref, block_ref, lane_ref):
    wide = jnp.concatenate(
        [wanted_ref[...].astype(F32), jnp.zeros((DEVICES, 128 - CAP), F32)], axis=1
    )
    wanted = wide.T[0:CAP].astype(I32)
    block_ref[...] = wanted >> 7
    lane_ref[...] = wanted & 127


def send_kernel(
    wanted_ref, screen_ref, ninth_ref, message_ref, row_ref, col_ref,
    block_ref, lane_ref, out_ref, out_ninth_ref, left_ref, right_ref,
):
    wanted_tables(wanted_ref, block_ref, lane_ref)
    gather(screen_ref, ninth_ref, block_ref, lane_ref, out_ref, out_ninth_ref, CAP, BLOCKS)
    pack_messages(out_ref, out_ninth_ref, message_ref)
    invert(block_ref, lane_ref, left_ref, right_ref, row_ref, col_ref, CAP, BLOCKS)


def lane_map(count_ref, place_ref):
    lane = lax.broadcasted_iota(I32, (1, 128), 1)
    tile = jnp.full((1, 128), -1, I32)
    segment = jnp.zeros((1, 128), I32)
    segments = jnp.zeros((1, 128), I32)
    count = jnp.zeros((1, 128), I32)
    origin_x = jnp.zeros((1, 128), I32)
    origin_y = jnp.zeros((1, 128), I32)
    base = jnp.int32(0)
    for index in range(TILES):
        listed = count_ref[0, index]
        place = place_ref[0, index]
        used = lax.div(listed + (SEG - 1), SEG)
        inside = (lane >= base) & (lane < base + used)
        place_y = lax.div(place, 120)
        tile = jnp.where(inside, index, tile)
        segment = jnp.where(inside, lane - base, segment)
        segments = jnp.where(inside, used, segments)
        count = jnp.where(inside, listed, count)
        origin_x = jnp.where(inside, 16 * (place - 120 * place_y), origin_x)
        origin_y = jnp.where(inside, 16 * place_y, origin_y)
        base = base + used
    return tile, segment, segments, count, origin_x, origin_y


def index_kernel(
    count_ref, place_ref, slots_ref,
    block_ref, lane_ref, row_ref, col_ref, lanes_ref, all_ref, left_ref, right_ref,
):
    tile, segment, segments, count, origin_x, origin_y = lane_map(count_ref, place_ref)
    lanes_ref[0:1] = tile
    lanes_ref[1:2] = segment
    lanes_ref[2:3] = segments
    lanes_ref[3:4] = count
    lanes_ref[4:5] = origin_x
    lanes_ref[5:6] = origin_y
    lanes_ref[6:8] = jnp.zeros((2, 128), I32)
    slots = slots_ref[...]
    owner = ((slots.astype(F32) + 0.5) * (1.0 / CAP)).astype(I32)
    within = slots - owner * CAP
    pick = jnp.where(
        lax.broadcasted_iota(I32, (TILES, 128), 0) == tile, 1.0, 0.0
    ).astype(jnp.bfloat16)
    contract = (((0,), (0,)), ((), ()))
    step = lax.broadcasted_iota(I32, (SEG_PAD, 128), 0)
    live = (step < SEG) & (step + segment * SEG < count)
    for values, out in ((within, block_ref), (owner, lane_ref)):
        all_ref[0:SLOTS] = lax.dot_general(
            values.astype(F32).astype(jnp.bfloat16), pick, contract, preferred_element_type=F32
        )
        all_ref[SLOTS:] = jnp.zeros_like(all_ref[SLOTS:])
        total = jnp.zeros((SEG_PAD, 128), F32)
        for part in range(SEGS):
            rows = all_ref[part * SEG : part * SEG + SEG_PAD]
            total = jnp.where(segment == part, rows, total)
        out[...] = jnp.where(live, (total + 0.5).astype(I32), -1)
    invert(block_ref, lane_ref, left_ref, right_ref, row_ref, col_ref, SEG, CAP)


def render_kernel(
    message_ref, block_ref, lane_ref, row_ref, col_ref, lanes_ref, target_ref,
    rendered_ref, gradient_ref,
    source_ref, source_ninth_ref, rows_ref, ninth_ref, pre_ref, alpha_ref, weight_ref,
    trans_ref, colour_ref, behind_ref, moment_ref, grad_ref, grad_ninth_ref,
    back_ref, back_ninth_ref,
):
    unpack_messages(message_ref, source_ref, source_ninth_ref)
    safe_lane_ref = lane_ref
    gather(
        source_ref, source_ninth_ref, block_ref, safe_lane_ref, rows_ref, ninth_ref, SEG, CAP
    )
    tile = lanes_ref[0:1]
    segment = lanes_ref[1:2]
    segments = lanes_ref[2:3]
    origin_x = lanes_ref[4:5].astype(F32)
    origin_y = lanes_ref[5:6].astype(F32)
    sub = lax.broadcasted_iota(I32, (8, 128), 0).astype(F32) + 0.5

    def wide(row):
        return jnp.broadcast_to(row, (8, 128))

    def prepare(step, carry):
        attrs = rows_ref[step]
        screen_x = attrs[0:1] - origin_x
        screen_y = attrs[1:2] - origin_y
        curve_x = wide(-0.5 * LOG2_E * attrs[2:3])
        curve_xy = wide(-LOG2_E * attrs[3:4])
        for half in range(2):
            delta = (sub + 8.0 * half) - wide(screen_x)
            pre_ref[step, half] = curve_x * delta * delta
            pre_ref[step, 2 + half] = curve_xy * delta
            pre_ref[step, 9 + half] = delta
        pre_ref[step, 4] = wide(screen_y)
        pre_ref[step, 5] = wide(-0.5 * LOG2_E * attrs[4:5])
        pre_ref[step, 6] = wide(attrs[5:6])
        pre_ref[step, 7] = wide(attrs[6:7])
        pre_ref[step, 8] = wide(attrs[7:8])
        pre_ref[step, 11] = wide(ninth_ref[pl.ds(step, 1), :])
        return carry

    lax.fori_loop(0, SEG, prepare, 0)

    def forward_pass(index, carry):
        first_v = (index * (GROUP // 2)).astype(F32) + 0.5

        def one_step(step, state):
            trans, red, green, blue = (list(part) for part in state)
            opacity, screen_y, curve_y = pre_ref[step, 6], pre_ref[step, 4], pre_ref[step, 5]
            colours = (pre_ref[step, 7], pre_ref[step, 8], pre_ref[step, 11])
            for pair in range(GROUP // 2):
                delta_y = (first_v + float(pair)) - screen_y
                bend = curve_y * delta_y * delta_y
                for half in range(2):
                    k = 2 * pair + half
                    power = pre_ref[step, half] + (bend + pre_ref[step, 2 + half] * delta_y)
                    alpha = opacity * jnp.exp2(power)
                    weight = alpha * trans[k]
                    trans[k] = trans[k] - weight
                    red[k] = red[k] + colours[0] * weight
                    green[k] = green[k] + colours[1] * weight
                    blue[k] = blue[k] + colours[2] * weight
                    alpha_ref[index, step, k] = alpha
                    weight_ref[index, step, k] = weight
            return tuple(trans), tuple(red), tuple(green), tuple(blue)

        ones = tuple(jnp.ones((8, 128), F32) for _ in range(GROUP))
        zeros = tuple(jnp.zeros((8, 128), F32) for _ in range(GROUP))
        state = lax.fori_loop(0, SEG, one_step, (ones, zeros, zeros, zeros))
        for k in range(GROUP):
            rows = pl.ds(pl.multiple_of((index * GROUP + k) * 8, 8), 8)
            trans_ref[rows, :] = state[0][k]
            for channel in range(3):
                colour_ref[channel, rows, :] = state[1 + channel][k]
        return carry

    lax.fori_loop(0, PASSES, forward_pass, 0)

    through = trans_ref[...]
    start = jnp.where(segment == 0, 1.0, pltpu.roll(through, 1, 1))
    for shift in (1, 2, 4, 8):
        start = start * jnp.where(segment >= shift, pltpu.roll(start, shift, 1), 1.0)
    pick = jnp.where(lax.broadcasted_iota(I32, (TILES, 128), 0) == tile, 1.0, 0.0)
    behind = jnp.zeros((256, 128), F32)
    for channel in range(3):
        image = lax.dot_general(
            pick, colour_ref[channel] * start, (((1,), (1,)), ((), ())),
            preferred_element_type=F32, precision=lax.Precision.HIGHEST,
        )
        rendered_ref[:, channel, :] = image
        error = (image - target_ref[:, channel, :]) * (1.0 / 256.0)
        spread = lax.dot_general(
            error, pick, (((0,), (0,)), ((), ())),
            preferred_element_type=F32, precision=lax.Precision.HIGHEST,
        )
        behind = behind + spread * colour_ref[channel]
        colour_ref[channel] = spread * start
    left = segments - 1 - segment
    factor = jnp.where(left >= 1, pltpu.roll(through, 127, 1), 0.0)
    behind = jnp.where(left >= 1, pltpu.roll(behind, 127, 1), 0.0)
    for shift in (1, 2, 4, 8):
        reach = left >= shift
        behind = behind + factor * jnp.where(reach, pltpu.roll(behind, 128 - shift, 1), 0.0)
        factor = factor * jnp.where(reach, pltpu.roll(factor, 128 - shift, 1), 0.0)
    behind_ref[...] = behind * start

    def clear(step, carry):
        for row in range(9):
            moment_ref[step, row] = jnp.zeros((8, 128), F32)
        return carry

    lax.fori_loop(0, SEG, clear, 0)

    def backward_pass(index, carry):
        first_v = (index * (GROUP // 2)).astype(F32) + 0.5
        rows = [pl.ds(pl.multiple_of((index * GROUP + k) * 8, 8), 8) for k in range(GROUP)]
        errors = [[colour_ref[channel, rows[k], :] for channel in range(3)] for k in range(GROUP)]

        def one_step(count, state):
            step = SEG - 1 - count
            state = list(state)
            screen_y = pre_ref[step, 4]
            colours = (pre_ref[step, 7], pre_ref[step, 8], pre_ref[step, 11])
            sums = [moment_ref[step, row] for row in range(9)]
            for pair in range(GROUP // 2):
                delta_y = (first_v + float(pair)) - screen_y
                for half in range(2):
                    k = 2 * pair + half
                    alpha = alpha_ref[index, step, k]
                    weight = weight_ref[index, step, k]
                    shade = (
                        colours[0] * errors[k][0]
                        + colours[1] * errors[k][1]
                        + colours[2] * errors[k][2]
                    )
                    gap = shade - state[k]
                    state[k] = state[k] + alpha * gap
                    slope = weight * gap
                    slope_y = slope * delta_y
                    sums[3 * half] = sums[3 * half] + slope
                    sums[3 * half + 1] = sums[3 * half + 1] + slope_y
                    sums[3 * half + 2] = sums[3 * half + 2] + slope_y * delta_y
                    for channel in range(3):
                        sums[6 + channel] = sums[6 + channel] + weight * errors[k][channel]
            for row in range(9):
                moment_ref[step, row] = sums[row]
            return tuple(state)

        lax.fori_loop(0, SEG, one_step, tuple(behind_ref[rows[k], :] for k in range(GROUP)))
        return carry

    lax.fori_loop(0, PASSES, backward_pass, 0)

    def finish(step, carry):
        delta = [pre_ref[step, 9], pre_ref[step, 10]]
        sums = [moment_ref[step, row] for row in range(9)]
        flat = [sums[0], sums[3]]
        tilt = [sums[1], sums[4]]
        bend = [sums[2], sums[5]]
        side = [flat[half] * delta[half] for half in range(2)]

        def total(register):
            return jnp.sum(register, axis=0, keepdims=True)

        m00 = total(flat[0] + flat[1])
        m10 = total(side[0] + side[1])
        m01 = total(tilt[0] + tilt[1])
        m20 = total(side[0] * delta[0] + side[1] * delta[1])
        m11 = total(tilt[0] * delta[0] + tilt[1] * delta[1])
        m02 = total(bend[0] + bend[1])
        attrs = rows_ref[step]
        conic_a, conic_b, conic_c = attrs[2:3], attrs[3:4], attrs[4:5]
        grad_ref[step] = jnp.concatenate(
            [
                conic_a * m10 + conic_b * m01,
                conic_b * m10 + conic_c * m01,
                -0.5 * m20,
                -m11,
                -0.5 * m02,
                m00,
                total(sums[6]),
                total(sums[7]),
            ],
            axis=0,
        )
        ninth_ref[pl.ds(step, 1), :] = total(sums[8])
        return carry

    lax.fori_loop(0, SEG, finish, 0)
    ninth_ref[SEG:SEG_PAD] = jnp.zeros((SEG_PAD - SEG, 128), F32)
    grad_ninth_ref[...] = ninth_ref[...].reshape(SEG_PAD // 8, 8, 128)
    gather(grad_ref, grad_ninth_ref, row_ref, col_ref, back_ref, back_ninth_ref, CAP, SEG)
    pack_messages(back_ref, back_ninth_ref, gradient_ref)


def pullback_kernel(
    message_ref, row_ref, col_ref, params_ref, gradient_ref,
    source_ref, source_ninth_ref, rows_ref, ninth_ref,
):
    unpack_messages(message_ref, source_ref, source_ninth_ref)
    gather(source_ref, source_ninth_ref, row_ref, col_ref, rows_ref, ninth_ref, BLOCKS, CAP)

    def one_group(group, carry):
        columns = pl.ds(pl.multiple_of(group * 1024, 1024), 1024)
        eight = pl.ds(pl.multiple_of(group * 8, 8), 8)
        rows = load_rows(params_ref, group)
        screen_grad = [rows_ref[eight, row, :] for row in range(8)] + [ninth_ref[eight, :]]
        screen, pullback = jax.vjp(project, rows)
        by_logit = screen_grad[5] * (1.0 / (1.0 + jnp.exp(rows[10])))
        screen_grad[5] = jnp.zeros_like(by_logit)
        (grads,) = pullback(screen_grad)
        grads[10] = by_logit
        for row in range(PARAMS):
            gradient_ref[row : row + 1, columns] = grads[row].reshape(1, 1024)
        return carry

    lax.fori_loop(0, OWNED // 1024, one_group, 0)


def shape(dims, dtype=F32):
    return jax.ShapeDtypeStruct(dims, dtype)


def call(kernel, outs, scratch, name, smem=0, operands=0):
    params = pltpu.CompilerParams(vmem_limit_bytes=VMEM_LIMIT)
    specs = [pl.BlockSpec(memory_space=pltpu.SMEM)] * smem
    specs += [pl.BlockSpec(memory_space=pltpu.VMEM)] * (operands - smem)
    return pl.pallas_call(
        kernel,
        out_shape=outs,
        in_specs=specs,
        out_specs=[pl.BlockSpec(memory_space=pltpu.VMEM)] * len(outs),
        scratch_shapes=scratch,
        compiler_params=params,
        name=name,
    )


MESSAGE = (DEVICES, 4, 128)
TABLE = (CAP, 128)
EIGHT = (CAP, 8, 128)
NINE = (CAP // 8, 8, 128)


def exchange(messages):
    return lax.all_to_all(messages, "dev", split_axis=0, concat_axis=0, tiled=True)


def exchange_requests(requests):
    return lax.all_to_all(requests, "dev", split_axis=1, concat_axis=0, tiled=True)


def local(params, requests, tile_slots, tile_count, tile_place, target):
    vmem = pltpu.VMEM
    wanted = exchange_requests(requests).reshape(DEVICES, CAP)
    screen, ninth = call(
        project_kernel, [shape(EIGHT), shape(NINE)], [], "project", operands=1
    )(params)
    messages, owner_row, owner_col = call(
        send_kernel,
        [shape(MESSAGE), shape(TABLE, I32), shape(TABLE, I32)],
        [
            vmem(TABLE, I32), vmem(TABLE, I32), vmem(EIGHT, F32), vmem(TABLE, F32),
            vmem((2 * BLOCKS, CAP * 128), jnp.bfloat16), vmem((128, CAP * 128), jnp.bfloat16),
        ],
        "send",
        operands=3,
    )(wanted, screen, ninth)
    received = exchange(messages)
    steps = (SEG_PAD, 128)
    block, lane, slot_row, slot_col, lanes = call(
        index_kernel,
        [
            shape(steps, I32), shape(steps, I32), shape(TABLE, I32), shape(TABLE, I32),
            shape((8, 128), I32),
        ],
        [
            vmem((SEGS * SEG + 8, 128), F32),
            vmem((2 * CAP, SEG * 128), jnp.bfloat16), vmem((128, SEG * 128), jnp.bfloat16),
        ],
        "index",
        smem=2,
        operands=3,
    )(tile_count.reshape(1, TILES), tile_place.reshape(1, TILES), tile_slots)
    rendered, gradients = call(
        render_kernel,
        [shape((TILES, 3, 256)), shape(MESSAGE)],
        [
            vmem(EIGHT, F32), vmem(NINE, F32),
            vmem((SEG, 8, 128), F32), vmem(steps, F32),
            vmem((SEG, 12, 8, 128), F32),
            vmem((PASSES, SEG, GROUP, 8, 128), F32), vmem((PASSES, SEG, GROUP, 8, 128), F32),
            vmem((256, 128), F32), vmem((3, 256, 128), F32), vmem((256, 128), F32),
            vmem((SEG, 9, 8, 128), F32),
            vmem((SEG, 8, 128), F32), vmem((SEG_PAD // 8, 8, 128), F32),
            vmem(EIGHT, F32), vmem(TABLE, F32),
        ],
        "render",
        operands=7,
    )(received, block, lane, slot_row, slot_col, lanes, target)
    returned = exchange(gradients)
    (gradient,) = call(
        pullback_kernel,
        [shape((PARAMS, OWNED))],
        [vmem(EIGHT, F32), vmem(NINE, F32), vmem(EIGHT, F32), vmem(TABLE, F32)],
        "pullback",
        operands=4,
    )(returned, owner_row, owner_col, params)
    return rendered, gradient


def solution(mesh):
    in_specs = (
        P(None, "dev"),
        P("dev", None, None),
        P("dev", None),
        P("dev"),
        P("dev"),
        P("dev", None, None),
    )
    out_specs = (P("dev", None, None), P(None, "dev"))
    return jax.shard_map(local, mesh=mesh, in_specs=in_specs, out_specs=out_specs, check_vma=False)
```

profile of v0, /device:TPU:1, one launch (start us, length us, event | category | flops | bytes accessed | tf_op | source)
XLA Modules:
  0.0 95.4 jit_solution(11652558249459215426)
XLA Ops:
  0.6 0.0 copy-start.5
  0.6 0.0 copy-start.4
  0.7 0.0 copy-start.3
  0.7 0.0 copy-start.2
  0.7 1.5 %copy.11 = s32[1,128,40]{2,0,1:T(1,128)} copy(s32[1,128,40]{1,2,0:T(8,128)} %param.7) | data formatting | bytes 40960 | tf_op args[1]
  2.2 11.5 %all-to-all-start = ((s32[1,128,40]{2,0,1:T(1,128)}), s32[1,128,40]{2,0,1:T(1,128)S(1)}, u32[]{:S(2)}, u32[]{:S(2)}) async-start(s32[1,128,40]{2,0,1:T(1,128)} %copy.11), calls=%async_computation | async-start | bytes 131072 | tf_op jit(solution)/shard_map/all_to_all | solution.py:520
  13.7 0.0 copy-start
  13.7 1.3 %copy-done = f32[59,5120]{1,0:T(8,128)S(1)} copy-done((f32[59,5120]{1,0:T(8,128)S(1)}, f32[59,5120]{1,0:T(8,128)}, u32[]{:S(2)}) %copy-start) | copy-done | bytes 1208344
  15.0 0.4 project.1
  15.4 0.0 copy-start.1
  15.4 7.6 %all-to-all-done = s32[1,128,40]{2,0,1:T(1,128)S(1)} async-done(((s32[1,128,40]{2,0,1:T(1,128)}), s32[1,128,40]{2,0,1:T(1,128)S(1)}, u32[]{:S(2)}, u32[]{:S(2)}) %all-to-all-start) | async-done | bytes 20512 | tf_op jit(solution)/shard_map/all_to_all | solution.py:520
  23.0 6.6 %send.1 = (f32[128,4,128]{2,1,0:T(4,128)}, s32[40,128]{1,0:T(8,128)S(1)}, s32[40,128]{1,0:T(8,128)S(1)}) custom-call(s32[128,40]{1,0:T(8,128)S(1)} %bitcast.3, f32[40,8,128]{2,1,0:T(8,128)S(1)} %get-tuple-element.14.screen_ref, f32[5,8,128]{2,1,0:T(8,128)S(1)} %get-tuple-element.15.ninth_ref), custom_call_target="tpu_custom_call" | custom-call | tf_op jit(solution)/shard_map/send/pallas_call | solution.py:529
  29.6 4.6 %all-to-all-start.1 = ((f32[128,4,128]{2,1,0:T(4,128)}), f32[128,4,128]{2,1,0:T(4,128)S(1)}, u32[]{:S(2)}, u32[]{:S(2)}) async-start(f32[128,4,128]{2,1,0:T(4,128)} %get-tuple-element.16), calls=%async_computation.1 | async-start | bytes 524288 | tf_op jit(solution)/shard_map/all_to_all | solution.py:516
  34.2 0.0 copy-done.5
  34.2 0.0 copy-done.4
  34.3 0.0 copy-done.3
  34.3 0.0 copy-done.2
  34.3 2.3 %index.1 = (s32[48,128]{1,0:T(8,128)S(1)}, s32[48,128]{1,0:T(8,128)S(1)}, s32[40,128]{1,0:T(8,128)S(1)}, s32[40,128]{1,0:T(8,128)S(1)}, s32[8,128]{1,0:T(8,128)S(1)}) custom-call(s32[1,16]{1,0:T(1,128)S(1)} %bitcast.4, s32[1,16]{1,0:T(1,128)S(1)} %bitcast.5, s32[16,512]{1,0:T(8,128)S(1)} %copy-done.2), custom_call_target="tpu_custom_call" | custom-call | tf_op jit(solution)/shard_map/index/pallas_call | solution.py:541
  36.6 8.6 %all-to-all-done.1.message_ref = f32[128,4,128]{2,1,0:T(4,128)S(1)} async-done(((f32[128,4,128]{2,1,0:T(4,128)}), f32[128,4,128]{2,1,0:T(4,128)S(1)}, u32[]{:S(2)}, u32[]{:S(2)}) %all-to-all-start.1) | async-done | bytes 262176 | tf_op jit(solution)/shard_map/all_to_all | solution.py:516
  45.2 27.7 %render.1 = (f32[16,3,256]{2,1,0:T(4,128)S(1)}, f32[128,4,128]{2,1,0:T(4,128)}) custom-call(f32[128,4,128]{2,1,0:T(4,128)S(1)} %all-to-all-done.1.message_ref, s32[48,128]{1,0:T(8,128)S(1)} %get-tuple-element.17.block_ref, s32[48,128]{1,0:T(8,128)S(1)} %get-tuple-element.18.lane_ref, s32[40,128]{1,0:T(8,128)S(1)} %get-tuple-element.19.row_ref, ...), custom_call_target="tpu_custom_call" | custom-call | tf_op jit(solution)/shard_map/render/pallas_call | solution.py:555
  72.9 4.5 %all-to-all-start.2 = ((f32[128,4,128]{2,1,0:T(4,128)}), f32[128,4,128]{2,1,0:T(4,128)S(1)}, u32[]{:S(2)}, u32[]{:S(2)}) async-start(f32[128,4,128]{2,1,0:T(4,128)} %get-tuple-element.23), calls=%async_computation.2 | async-start | bytes 524288 | tf_op jit(solution)/shard_map/all_to_all | solution.py:516
  77.5 0.6 copy.13
  78.1 10.4 %all-to-all-done.2.message_ref = f32[128,4,128]{2,1,0:T(4,128)S(1)} async-done(((f32[128,4,128]{2,1,0:T(4,128)}), f32[128,4,128]{2,1,0:T(4,128)S(1)}, u32[]{:S(2)}, u32[]{:S(2)}) %all-to-all-start.2) | async-done | bytes 262176 | tf_op jit(solution)/shard_map/all_to_all | solution.py:516
  88.5 0.0 copy-done.1
  88.5 7.0 %pullback.1 = f32[59,5120]{1,0:T(8,128)} custom-call(f32[128,4,128]{2,1,0:T(4,128)S(1)} %all-to-all-done.2.message_ref, s32[40,128]{1,0:T(8,128)S(1)} %get-tuple-element.24.row_ref, s32[40,128]{1,0:T(8,128)S(1)} %get-tuple-element.25.col_ref, f32[59,5120]{1,0:T(8,128)S(1)} %copy-done.1), custom_call_target="tpu_custom_call" | custom-call | tf_op jit(solution)/shard_map/pullback/pallas_call | solution.py:572
  (1 shorter events, 0.0 us)
Async XLA Ops:
  0.6 33.6 %copy-start.5 = (f32[16,3,256]{2,0,1:T(8,128)S(1)}, f32[16,3,256]{2,0,1:T(8,128)}, u32[]{:S(2)}) copy-start(f32[16,3,256]{2,0,1:T(8,128)} %param.11) | copy-start | bytes 147460
  0.6 33.6 %copy-start.4 = (s32[16]{0:T(128)S(1)}, s32[16]{0:T(128)}, u32[]{:S(2)}) copy-start(s32[16]{0:T(128)} %param.10) | copy-start | bytes 196
  0.7 33.6 %copy-start.3 = (s32[16]{0:T(128)S(1)}, s32[16]{0:T(128)}, u32[]{:S(2)}) copy-start(s32[16]{0:T(128)} %param.9) | copy-start | bytes 196
  0.7 33.6 %copy-start.2 = (s32[16,512]{1,0:T(8,128)S(1)}, s32[16,512]{1,0:T(8,128)}, u32[]{:S(2)}) copy-start(s32[16,512]{1,0:T(8,128)} %slots_ref.1) | copy-start | bytes 98308
  2.2 20.8 %all-to-all-start = ((s32[1,128,40]{2,0,1:T(1,128)}), s32[1,128,40]{2,0,1:T(1,128)S(1)}, u32[]{:S(2)}, u32[]{:S(2)}) async-start(s32[1,128,40]{2,0,1:T(1,128)} %copy.11), calls=%async_computation | async-start | bytes 131072 | tf_op jit(solution)/shard_map/all_to_all | solution.py:520
  13.7 1.3 %copy-start = (f32[59,5120]{1,0:T(8,128)S(1)}, f32[59,5120]{1,0:T(8,128)}, u32[]{:S(2)}) copy-start(f32[59,5120]{1,0:T(8,128)} %params_ref.3) | copy-start | bytes 3624964
  15.4 73.1 %copy-start.1 = (f32[59,5120]{1,0:T(8,128)S(1)}, f32[59,5120]{1,0:T(8,128)}, u32[]{:S(2)}) copy-start(f32[59,5120]{1,0:T(8,128)} %params_ref.3) | copy-start | bytes 3624964
  29.6 15.6 %all-to-all-start.1 = ((f32[128,4,128]{2,1,0:T(4,128)}), f32[128,4,128]{2,1,0:T(4,128)S(1)}, u32[]{:S(2)}, u32[]{:S(2)}) async-start(f32[128,4,128]{2,1,0:T(4,128)} %get-tuple-element.16), calls=%async_computation.1 | async-start | bytes 524288 | tf_op jit(solution)/shard_map/all_to_all | solution.py:516
  72.9 15.6 %all-to-all-start.2 = ((f32[128,4,128]{2,1,0:T(4,128)}), f32[128,4,128]{2,1,0:T(4,128)S(1)}, u32[]{:S(2)}, u32[]{:S(2)}) async-start(f32[128,4,128]{2,1,0:T(4,128)} %get-tuple-element.23), calls=%async_computation.2 | async-start | bytes 524288 | tf_op jit(solution)/shard_map/all_to_all | solution.py:516
where the time goes:
time: 95.7 us; the launch traced here: 95.4 us
  Pallas kernels  44 us (46%)
  waiting for transfers between devices  26.6 us (28%)
  starting transfers between devices  20.6 us (22%)
  local copies, waits for them, and re-layouts  3.49 us (4%)
    pallas_call x1, Pallas kernels, local(): call(render_kernel, [shape((TILES, 3, 256)), shape(MESSAGE)], [vmem(EIGHT...  27.7 us
    all_to_all x2, waiting for transfers between devices, exchange(): lax.all_to_all(messages, 'dev', split_axis=0, concat_axis=0, tiled=True)  19 us
    all_to_all x1, starting transfers between devices, exchange_requests(): lax.all_to_all(requests, 'dev', split_axis=1, concat_axis=0, tiled=True)  11.5 us
    all_to_all x2, starting transfers between devices, exchange(): lax.all_to_all(messages, 'dev', split_axis=0, concat_axis=0, tiled=True)  9.14 us
    all_to_all x1, waiting for transfers between devices, exchange_requests(): lax.all_to_all(requests, 'dev', split_axis=1, concat_axis=0, tiled=True)  7.57 us
    pallas_call x1, Pallas kernels, local(): call(pullback_kernel, [shape((PARAMS, OWNED))], [vmem(EIGHT, F32), vmem(N...  6.96 us
    pallas_call x1, Pallas kernels, local(): call(send_kernel, [shape(MESSAGE), shape(TABLE, I32), shape(TABLE, I32)],...  6.59 us
    unnamed x15, local copies, waits for them, and re-layouts  3.49 us
  transfers between devices with their start and end apart: 3, of which 3 were waited for; matrix products, arithmetic and copies ran while one was open for 1% of the time, Pallas kernels for 3%

commit v1 on v0

--- a/solution.py
+++ b/solution.py
@@ -43,6 +43,10 @@
 SEGS = 12
 GROUP = 8
 PASSES = 32 // GROUP
+STEP_UNROLL = 2
+BACK_UNROLL = 2
+SHORT_UNROLL = 23
+BF16 = jnp.bfloat16
 F32 = jnp.float32
 I32 = jnp.int32
 VMEM_LIMIT = 48 * 1024 * 1024
@@ -123,26 +127,94 @@
     lax.fori_loop(0, OWNED // 1024, one_group, 0)
 
 
-def gather(source_ref, ninth_ref, block_ref, lane_ref, out_ref, out_ninth_ref, targets, sources):
+def repeat(count, unroll, body, state):
+    def turn(index, state):
+        for part in range(unroll):
+            state = body(index * unroll + part, state)
+        return state
+
+    return lax.fori_loop(0, count // unroll, turn, state)
+
+
+def gather(
+    source_ref, ninth_ref, block_ref, lane_ref, out_ref, out_ninth_ref, split_ref,
+    targets, sources, by_matmul, by_lanes,
+):
+    half = sources // 2
+    eights = half * 8
+    height = eights + 24
+    width = 128 * by_matmul
+    ninth = ninth_ref[...].reshape(-1, 128)
+    rest = jnp.concatenate(
+        [
+            jnp.concatenate([ninth[0:half], ninth[half:sources]], axis=1),
+            jnp.zeros((24 - half, 256), F32),
+        ],
+        axis=0,
+    )
+    main = jnp.concatenate(
+        [
+            source_ref[0:half].reshape(eights, 128),
+            source_ref[half:sources].reshape(eights, 128),
+        ],
+        axis=1,
+    )
+    for part in range(3):
+        for values, start in ((main, 0), (rest, eights)):
+            rounded = values.astype(BF16)
+            split_ref[part * height + start : part * height + start + values.shape[0]] = rounded
+        main = main - main.astype(BF16).astype(F32)
+        rest = rest - rest.astype(BF16).astype(F32)
+    iota = lax.broadcasted_iota(I32, (256, width), 0).astype(F32).astype(BF16)
+    sublane_rest = lax.broadcasted_iota(I32, (24, width), 0)
     sublane = lax.broadcasted_iota(I32, (8, 128), 0)
 
-    def one_row(row, carry):
-        lane = jnp.broadcast_to(lane_ref[pl.ds(row, 1), :], (8, 128))
-        block = jnp.broadcast_to(block_ref[pl.ds(row, 1), :], (8, 128))
-        total = jnp.zeros((8, 128), F32)
-        for source in range(sources):
-            picked = jnp.take_along_axis(source_ref[source], lane, axis=1)
-            total = jnp.where(block == source, picked, total)
-        out_ref[row] = total
-        place = block - sublane
-        total = jnp.zeros((8, 128), F32)
-        for source in range((sources + 7) // 8):
-            picked = jnp.take_along_axis(ninth_ref[source], lane, axis=1)
-            total = jnp.where(place == 8 * source, picked, total)
-        out_ninth_ref[pl.ds(row, 1), :] = jnp.sum(total, axis=0, keepdims=True)
+    def turn(index, carry):
+        base = index * (by_matmul + by_lanes)
+        rows = [pl.ds(base + k, 1) for k in range(by_matmul)]
+        block = jnp.concatenate([block_ref[row, :] for row in rows], axis=1)
+        lane = jnp.concatenate([lane_ref[row, :] for row in rows], axis=1)
+        upper = jnp.where(block >= half, 1, 0)
+        key = jnp.broadcast_to((lane + 128 * upper).astype(F32), (16, width)).astype(BF16)
+        place = block - half * upper
+        match = jnp.concatenate([key] * 16, axis=0) == iota
+        pick = jnp.where(match, jnp.ones((), BF16), jnp.zeros((), BF16))
+        parts = lax.dot_general(
+            split_ref[...], pick, (((1,), (0,)), ((), ())), preferred_element_type=F32
+        )
+        for k in range(by_lanes):
+            row = base + by_matmul + k
+            lane = jnp.broadcast_to(lane_ref[pl.ds(row, 1), :], (8, 128))
+            block = jnp.broadcast_to(block_ref[pl.ds(row, 1), :], (8, 128))
+            total = jnp.zeros((8, 128), F32)
+            for source in range(sources):
+                picked = jnp.take_along_axis(
+                    source_ref[source], lane, axis=1, mode="promise_in_bounds"
+                )
+                total = jnp.where(block == source, picked, total)
+            out_ref[row] = total
+            offset = block - sublane
+            total = jnp.zeros((8, 128), F32)
+            for source in range((sources + 7) // 8):
+                picked = jnp.take_along_axis(
+                    ninth_ref[source], lane, axis=1, mode="promise_in_bounds"
+                )
+                total = jnp.where(offset == 8 * source, picked, total)
+            out_ninth_ref[pl.ds(row, 1), :] = jnp.sum(total, axis=0, keepdims=True)
+        values = (parts[0:height] + parts[height : 2 * height]) + parts[2 * height : 3 * height]
+        wide = jnp.broadcast_to(place, (8, width))
+        total = jnp.zeros((8, width), F32)
+        for source in range(half):
+            total = jnp.where(wide == source, values[8 * source : 8 * source + 8], total)
+        last = jnp.sum(
+            jnp.where(sublane_rest == place, values[eights:height], 0.0), axis=0, keepdims=True
+        )
+        for k in range(by_matmul):
+            out_ref[base + k] = total[:, 128 * k : 128 * k + 128]
+            out_ninth_ref[pl.ds(base + k, 1), :] = last[:, 128 * k : 128 * k + 128]
         return carry
 
-    lax.fori_loop(0, targets, one_row, 0)
+    lax.fori_loop(0, targets // (by_matmul + by_lanes), turn, 0)
 
 
 def invert(block_ref, lane_ref, left_ref, right_ref, row_ref, col_ref, rows, blocks):
@@ -154,16 +226,16 @@
         columns = pl.ds(pl.multiple_of(row * 128, 128), 128)
         here = iota_block == block_ref[pl.ds(row, 1), :]
         value = jnp.full((1, 128), 0.0, F32) + row.astype(F32)
-        left_ref[0:blocks, columns] = jnp.where(here, value, 0.0).astype(jnp.bfloat16)
+        left_ref[0:blocks, columns] = jnp.where(here, value, 0.0).astype(BF16)
         left_ref[blocks : 2 * blocks, columns] = jnp.where(here, iota_lane, 0.0).astype(
-            jnp.bfloat16
+            BF16
         )
         right_ref[:, columns] = jnp.where(
             iota_sub == lane_ref[pl.ds(row, 1), :], 1.0, 0.0
-        ).astype(jnp.bfloat16)
+        ).astype(BF16)
         return carry
 
-    lax.fori_loop(0, rows, one_row, 0)
+    repeat(rows, 2, one_row, 0)
     found = lax.dot_general(
         left_ref[...], right_ref[...], (((1,), (1,)), ((), ())), preferred_element_type=F32
     )
@@ -200,12 +272,18 @@
 
 
 def send_kernel(
-    wanted_ref, screen_ref, ninth_ref, message_ref, row_ref, col_ref,
-    block_ref, lane_ref, out_ref, out_ninth_ref, left_ref, right_ref,
+    wanted_ref, screen_ref, ninth_ref, message_ref, block_ref, lane_ref,
+    out_ref, out_ninth_ref, split_ref,
 ):
     wanted_tables(wanted_ref, block_ref, lane_ref)
-    gather(screen_ref, ninth_ref, block_ref, lane_ref, out_ref, out_ninth_ref, CAP, BLOCKS)
+    gather(
+        screen_ref, ninth_ref, block_ref, lane_ref, out_ref, out_ninth_ref, split_ref,
+        CAP, BLOCKS, 10, 10,
+    )
     pack_messages(out_ref, out_ninth_ref, message_ref)
+
+
+def invert_kernel(block_ref, lane_ref, row_ref, col_ref, left_ref, right_ref):
     invert(block_ref, lane_ref, left_ref, right_ref, row_ref, col_ref, CAP, BLOCKS)
 
 
@@ -251,20 +329,20 @@
     within = slots - owner * CAP
     pick = jnp.where(
         lax.broadcasted_iota(I32, (TILES, 128), 0) == tile, 1.0, 0.0
-    ).astype(jnp.bfloat16)
+    ).astype(BF16)
     contract = (((0,), (0,)), ((), ()))
     step = lax.broadcasted_iota(I32, (SEG_PAD, 128), 0)
     live = (step < SEG) & (step + segment * SEG < count)
-    for values, out in ((within, block_ref), (owner, lane_ref)):
+    for values, out, unused in ((within, block_ref, -1), (owner, lane_ref, 0)):
         all_ref[0:SLOTS] = lax.dot_general(
-            values.astype(F32).astype(jnp.bfloat16), pick, contract, preferred_element_type=F32
+            values.astype(F32).astype(BF16), pick, contract, preferred_element_type=F32
         )
         all_ref[SLOTS:] = jnp.zeros_like(all_ref[SLOTS:])
         total = jnp.zeros((SEG_PAD, 128), F32)
         for part in range(SEGS):
             rows = all_ref[part * SEG : part * SEG + SEG_PAD]
             total = jnp.where(segment == part, rows, total)
-        out[...] = jnp.where(live, (total + 0.5).astype(I32), -1)
+        out[...] = jnp.where(live, (total + 0.5).astype(I32), unused)
     invert(block_ref, lane_ref, left_ref, right_ref, row_ref, col_ref, SEG, CAP)
 
 
@@ -273,12 +351,12 @@
     rendered_ref, gradient_ref,
     source_ref, source_ninth_ref, rows_ref, ninth_ref, pre_ref, alpha_ref, weight_ref,
     trans_ref, colour_ref, behind_ref, moment_ref, grad_ref, grad_ninth_ref,
-    back_ref, back_ninth_ref,
+    back_ref, back_ninth_ref, split_ref, split_back_ref,
 ):
     unpack_messages(message_ref, source_ref, source_ninth_ref)
-    safe_lane_ref = lane_ref
     gather(
-        source_ref, source_ninth_ref, block_ref, safe_lane_ref, rows_ref, ninth_ref, SEG, CAP
+        source_ref, source_ninth_ref, block_ref, lane_ref, rows_ref, ninth_ref, split_ref,
+        SEG, CAP, 12, 11,
     )
     tile = lanes_ref[0:1]
     segment = lanes_ref[1:2]
@@ -309,10 +387,10 @@
         pre_ref[step, 11] = wide(ninth_ref[pl.ds(step, 1), :])
         return carry
 
-    lax.fori_loop(0, SEG, prepare, 0)
-
-    def forward_pass(index, carry):
-        first_v = (index * (GROUP // 2)).astype(F32) + 0.5
+    repeat(SEG, SHORT_UNROLL, prepare, 0)
+
+    for index in range(PASSES):
+        first_v = index * (GROUP // 2) + 0.5
 
         def one_step(step, state):
             trans, red, green, blue = (list(part) for part in state)
@@ -336,15 +414,12 @@
 
         ones = tuple(jnp.ones((8, 128), F32) for _ in range(GROUP))
         zeros = tuple(jnp.zeros((8, 128), F32) for _ in range(GROUP))
-        state = lax.fori_loop(0, SEG, one_step, (ones, zeros, zeros, zeros))
+        state = repeat(SEG, STEP_UNROLL, one_step, (ones, zeros, zeros, zeros))
         for k in range(GROUP):
-            rows = pl.ds(pl.multiple_of((index * GROUP + k) * 8, 8), 8)
+            rows = pl.ds((index * GROUP + k) * 8, 8)
             trans_ref[rows, :] = state[0][k]
             for channel in range(3):
                 colour_ref[channel, rows, :] = state[1 + channel][k]
-        return carry
-
-    lax.fori_loop(0, PASSES, forward_pass, 0)
 
     through = trans_ref[...]
     start = jnp.where(segment == 0, 1.0, pltpu.roll(through, 1, 1))
@@ -374,16 +449,9 @@
         factor = factor * jnp.where(reach, pltpu.roll(factor, 128 - shift, 1), 0.0)
     behind_ref[...] = behind * start
 
-    def clear(step, carry):
-        for row in range(9):
-            moment_ref[step, row] = jnp.zeros((8, 128), F32)
-        return carry
-
-    lax.fori_loop(0, SEG, clear, 0)
-
-    def backward_pass(index, carry):
-        first_v = (index * (GROUP // 2)).astype(F32) + 0.5
-        rows = [pl.ds(pl.multiple_of((index * GROUP + k) * 8, 8), 8) for k in range(GROUP)]
+    for index in range(PASSES):
+        first_v = index * (GROUP // 2) + 0.5
+        rows = [pl.ds((index * GROUP + k) * 8, 8) for k in range(GROUP)]
         errors = [[colour_ref[channel, rows[k], :] for channel in range(3)] for k in range(GROUP)]
 
         def one_step(count, state):
@@ -391,7 +459,11 @@
             state = list(state)
             screen_y = pre_ref[step, 4]
             colours = (pre_ref[step, 7], pre_ref[step, 8], pre_ref[step, 11])
-            sums = [moment_ref[step, row] for row in range(9)]
+            sums = [moment_ref[step, row] if index else None for row in range(9)]
+
+            def add(row, value):
+                sums[row] = value if sums[row] is None else sums[row] + value
+
             for pair in range(GROUP // 2):
                 delta_y = (first_v + float(pair)) - screen_y
                 for half in range(2):
@@ -407,19 +479,18 @@
                     state[k] = state[k] + alpha * gap
                     slope = weight * gap
                     slope_y = slope * delta_y
-                    sums[3 * half] = sums[3 * half] + slope
-                    sums[3 * half + 1] = sums[3 * half + 1] + slope_y
-                    sums[3 * half + 2] = sums[3 * half + 2] + slope_y * delta_y
+                    add(3 * half, slope)
+                    add(3 * half + 1, slope_y)
+                    add(3 * half + 2, slope_y * delta_y)
                     for channel in range(3):
-                        sums[6 + channel] = sums[6 + channel] + weight * errors[k][channel]
+                        add(6 + channel, weight * errors[k][channel])
             for row in range(9):
                 moment_ref[step, row] = sums[row]
             return tuple(state)
 
-        lax.fori_loop(0, SEG, one_step, tuple(behind_ref[rows[k], :] for k in range(GROUP)))
-        return carry
-
-    lax.fori_loop(0, PASSES, backward_pass, 0)
+        repeat(
+            SEG, BACK_UNROLL, one_step, tuple(behind_ref[rows[k], :] for k in range(GROUP))
+        )
 
     def finish(step, carry):
         delta = [pre_ref[step, 9], pre_ref[step, 10]]
@@ -456,19 +527,25 @@
         ninth_ref[pl.ds(step, 1), :] = total(sums[8])
         return carry
 
-    lax.fori_loop(0, SEG, finish, 0)
+    repeat(SEG, SHORT_UNROLL, finish, 0)
     ninth_ref[SEG:SEG_PAD] = jnp.zeros((SEG_PAD - SEG, 128), F32)
     grad_ninth_ref[...] = ninth_ref[...].reshape(SEG_PAD // 8, 8, 128)
-    gather(grad_ref, grad_ninth_ref, row_ref, col_ref, back_ref, back_ninth_ref, CAP, SEG)
+    gather(
+        grad_ref, grad_ninth_ref, row_ref, col_ref, back_ref, back_ninth_ref, split_back_ref,
+        CAP, SEG, 10, 10,
+    )
     pack_messages(back_ref, back_ninth_ref, gradient_ref)
 
 
 def pullback_kernel(
     message_ref, row_ref, col_ref, params_ref, gradient_ref,
-    source_ref, source_ninth_ref, rows_ref, ninth_ref,
+    source_ref, source_ninth_ref, rows_ref, ninth_ref, split_ref,
 ):
     unpack_messages(message_ref, source_ref, source_ninth_ref)
-    gather(source_ref, source_ninth_ref, row_ref, col_ref, rows_ref, ninth_ref, BLOCKS, CAP)
+    gather(
+        source_ref, source_ninth_ref, row_ref, col_ref, rows_ref, ninth_ref, split_ref,
+        BLOCKS, CAP, 10, 10,
+    )
 
     def one_group(group, carry):
         columns = pl.ds(pl.multiple_of(group * 1024, 1024), 1024)
@@ -506,6 +583,8 @@
     )
 
 
+SPLIT = (3 * (CAP // 2 * 8 + 24), 256)
+SPLIT_BACK = (3 * (SEG // 2 * 8 + 24), 256)
 MESSAGE = (DEVICES, 4, 128)
 TABLE = (CAP, 128)
 EIGHT = (CAP, 8, 128)
@@ -526,17 +605,21 @@
     screen, ninth = call(
         project_kernel, [shape(EIGHT), shape(NINE)], [], "project", operands=1
     )(params)
-    messages, owner_row, owner_col = call(
+    messages, wanted_block, wanted_lane = call(
         send_kernel,
         [shape(MESSAGE), shape(TABLE, I32), shape(TABLE, I32)],
-        [
-            vmem(TABLE, I32), vmem(TABLE, I32), vmem(EIGHT, F32), vmem(TABLE, F32),
-            vmem((2 * BLOCKS, CAP * 128), jnp.bfloat16), vmem((128, CAP * 128), jnp.bfloat16),
-        ],
+        [vmem(EIGHT, F32), vmem(TABLE, F32), vmem(SPLIT, BF16)],
         "send",
         operands=3,
     )(wanted, screen, ninth)
     received = exchange(messages)
+    owner_row, owner_col = call(
+        invert_kernel,
+        [shape(TABLE, I32), shape(TABLE, I32)],
+        [vmem((2 * BLOCKS, CAP * 128), BF16), vmem((128, CAP * 128), BF16)],
+        "invert",
+        operands=2,
+    )(wanted_block, wanted_lane)
     steps = (SEG_PAD, 128)
     block, lane, slot_row, slot_col, lanes = call(
         index_kernel,
@@ -546,7 +629,7 @@
         ],
         [
             vmem((SEGS * SEG + 8, 128), F32),
-            vmem((2 * CAP, SEG * 128), jnp.bfloat16), vmem((128, SEG * 128), jnp.bfloat16),
+            vmem((2 * CAP, SEG * 128), BF16), vmem((128, SEG * 128), BF16),
         ],
         "index",
         smem=2,
@@ -563,7 +646,7 @@
             vmem((256, 128), F32), vmem((3, 256, 128), F32), vmem((256, 128), F32),
             vmem((SEG, 9, 8, 128), F32),
             vmem((SEG, 8, 128), F32), vmem((SEG_PAD // 8, 8, 128), F32),
-            vmem(EIGHT, F32), vmem(TABLE, F32),
+            vmem(EIGHT, F32), vmem(TABLE, F32), vmem(SPLIT, BF16), vmem(SPLIT_BACK, BF16),
         ],
         "render",
         operands=7,
@@ -572,7 +655,10 @@
     (gradient,) = call(
         pullback_kernel,
         [shape((PARAMS, OWNED))],
-        [vmem(EIGHT, F32), vmem(NINE, F32), vmem(EIGHT, F32), vmem(TABLE, F32)],
+        [
+            vmem(EIGHT, F32), vmem(NINE, F32), vmem(EIGHT, F32), vmem(TABLE, F32),
+            vmem(SPLIT, BF16),
+        ],
         "pullback",
         operands=4,
     )(returned, owner_row, owner_col, params)

time: 95.7 us -> 76.2 us (0.80)
  Pallas kernels: 44 us -> 25.7 us
  waiting for transfers between devices: 26.6 us -> 25.3 us
    pallas_call x1, Pallas kernels: 27.7 us -> 16.1 us  [local(): call(render_kernel, [shape((TILES, 3, 256)), shape(MESSAGE)], [vmem(EIGHT...]
    pallas_call x1, Pallas kernels: 6.59 us -> 2.23 us  [local(): call(send_kernel, [shape(MESSAGE), shape(TABLE, I32), shape(TABLE, I32)],...]
    pallas_call x1, Pallas kernels: 6.96 us -> 3.41 us  [local(): call(pullback_kernel, [shape((PARAMS, OWNED))], [vmem(EIGHT, F32), vmem(N...]
    pallas_call x0 -> x1, Pallas kernels: none -> 1.25 us  [local(): call(invert_kernel, [shape(TABLE, I32), shape(TABLE, I32)], [vmem((2 * BL...]
    all_to_all x2, waiting for transfers between devices: 19 us -> 17.7 us  [exchange(): lax.all_to_all(messages, 'dev', split_axis=0, concat_axis=0, tiled=True)]
  transfers between devices with their start and end apart: 3 -> 3, of which waited for: 3 -> 3; matrix products, arithmetic and copies ran while one was open for 1% -> 1% of each run, Pallas kernels for 3% -> 5%
where the time goes in v1:
time: 76.2 us; the launch traced here: 75.9 us
  Pallas kernels  25.7 us (34%)
  waiting for transfers between devices  25.3 us (33%)
  starting transfers between devices  20.6 us (27%)
  local copies, waits for them, and re-layouts  3.5 us (5%)
    all_to_all x2, waiting for transfers between devices, exchange(): lax.all_to_all(messages, 'dev', split_axis=0, concat_axis=0, tiled=True)  17.7 us
    pallas_call x1, Pallas kernels, local(): call(render_kernel, [shape((TILES, 3, 256)), shape(MESSAGE)], [vmem(EIGHT...  16.1 us
    all_to_all x1, starting transfers between devices, exchange_requests(): lax.all_to_all(requests, 'dev', split_axis=1, concat_axis=0, tiled=True)  11.5 us
    all_to_all x2, starting transfers between devices, exchange(): lax.all_to_all(messages, 'dev', split_axis=0, concat_axis=0, tiled=True)  9.15 us
    all_to_all x1, waiting for transfers between devices, exchange_requests(): lax.all_to_all(requests, 'dev', split_axis=1, concat_axis=0, tiled=True)  7.57 us
    unnamed x15, local copies, waits for them, and re-layouts  3.5 us
    pallas_call x1, Pallas kernels, local(): call(pullback_kernel, [shape((PARAMS, OWNED))], [vmem(EIGHT, F32), vmem(N...  3.41 us
    pallas_call x1, Pallas kernels, local(): call(index_kernel, [shape(steps, I32), shape(steps, I32), shape(TABLE, I3...  2.28 us
  transfers between devices with their start and end apart: 3, of which 3 were waited for; matrix products, arithmetic and copies ran while one was open for 1% of the time, Pallas kernels for 5%

profile of v1, /device:TPU:1, one launch (start us, length us, event | category | flops | bytes accessed | tf_op | source)
XLA Modules:
  0.0 75.9 jit_solution(16388061251852200167)
XLA Ops:
  0.6 0.0 copy-start.5
  0.6 0.0 copy-start.4
  0.7 0.0 copy-start.3
  0.7 0.0 copy-start.2
  0.7 1.5 %copy.11 = s32[1,128,40]{2,0,1:T(1,128)} copy(s32[1,128,40]{1,2,0:T(8,128)} %param.7) | data formatting | bytes 40960 | tf_op args[1]
  2.2 11.5 %all-to-all-start = ((s32[1,128,40]{2,0,1:T(1,128)}), s32[1,128,40]{2,0,1:T(1,128)S(1)}, u32[]{:S(2)}, u32[]{:S(2)}) async-start(s32[1,128,40]{2,0,1:T(1,128)} %copy.11), calls=%async_computation | async-start | bytes 131072 | tf_op jit(solution)/shard_map/all_to_all | solution.py:599
  13.7 0.0 copy-start
  13.7 1.3 %copy-done = f32[59,5120]{1,0:T(8,128)S(1)} copy-done((f32[59,5120]{1,0:T(8,128)S(1)}, f32[59,5120]{1,0:T(8,128)}, u32[]{:S(2)}) %copy-start) | copy-done | bytes 1208344
  15.0 0.4 project.1
  15.4 0.0 copy-start.1
  15.4 7.6 %all-to-all-done = s32[1,128,40]{2,0,1:T(1,128)S(1)} async-done(((s32[1,128,40]{2,0,1:T(1,128)}), s32[1,128,40]{2,0,1:T(1,128)S(1)}, u32[]{:S(2)}, u32[]{:S(2)}) %all-to-all-start) | async-done | bytes 20512 | tf_op jit(solution)/shard_map/all_to_all | solution.py:599
  23.0 2.2 %send.1 = (f32[128,4,128]{2,1,0:T(4,128)}, s32[40,128]{1,0:T(8,128)S(1)}, s32[40,128]{1,0:T(8,128)S(1)}) custom-call(s32[128,40]{1,0:T(8,128)S(1)} %bitcast.3, f32[40,8,128]{2,1,0:T(8,128)S(1)} %get-tuple-element.16.screen_ref, f32[5,8,128]{2,1,0:T(8,128)S(1)} %get-tuple-element.17.ninth_ref), custom_call_target="tpu_custom_call" | custom-call | tf_op jit(solution)/shard_map/send/pallas_call | solution.py:608
  25.2 4.6 %all-to-all-start.1 = ((f32[128,4,128]{2,1,0:T(4,128)}), f32[128,4,128]{2,1,0:T(4,128)S(1)}, u32[]{:S(2)}, u32[]{:S(2)}) async-start(f32[128,4,128]{2,1,0:T(4,128)} %get-tuple-element.18), calls=%async_computation.1 | async-start | bytes 524288 | tf_op jit(solution)/shard_map/all_to_all | solution.py:595
  29.8 0.0 copy-done.5
  29.9 0.0 copy-done.4
  29.9 0.0 copy-done.3
  29.9 0.0 copy-done.2
  29.9 2.3 %index.1 = (s32[48,128]{1,0:T(8,128)S(1)}, s32[48,128]{1,0:T(8,128)S(1)}, s32[40,128]{1,0:T(8,128)S(1)}, s32[40,128]{1,0:T(8,128)S(1)}, s32[8,128]{1,0:T(8,128)S(1)}) custom-call(s32[1,16]{1,0:T(1,128)S(1)} %bitcast.4, s32[1,16]{1,0:T(1,128)S(1)} %bitcast.5, s32[16,512]{1,0:T(8,128)S(1)} %copy-done.2), custom_call_target="tpu_custom_call" | custom-call | tf_op jit(solution)/shard_map/index/pallas_call | solution.py:624
  32.2 8.6 %all-to-all-done.1.message_ref = f32[128,4,128]{2,1,0:T(4,128)S(1)} async-done(((f32[128,4,128]{2,1,0:T(4,128)}), f32[128,4,128]{2,1,0:T(4,128)S(1)}, u32[]{:S(2)}, u32[]{:S(2)}) %all-to-all-start.1) | async-done | bytes 262176 | tf_op jit(solution)/shard_map/all_to_all | solution.py:595
  40.8 16.1 %render.1 = (f32[16,3,256]{2,1,0:T(4,128)S(1)}, f32[128,4,128]{2,1,0:T(4,128)}) custom-call(f32[128,4,128]{2,1,0:T(4,128)S(1)} %all-to-all-done.1.message_ref, s32[48,128]{1,0:T(8,128)S(1)} %get-tuple-element.19.block_ref, s32[48,128]{1,0:T(8,128)S(1)} %get-tuple-element.20.lane_ref, s32[40,128]{1,0:T(8,128)S(1)} %get-tuple-element.21.row_ref, ...), custom_call_target="tpu_custom_call" | custom-call | tf_op jit(solution)/shard_map/render/pallas_call | solution.py:638
  56.9 4.5 %all-to-all-start.2 = ((f32[128,4,128]{2,1,0:T(4,128)}), f32[128,4,128]{2,1,0:T(4,128)S(1)}, u32[]{:S(2)}, u32[]{:S(2)}) async-start(f32[128,4,128]{2,1,0:T(4,128)} %get-tuple-element.25), calls=%async_computation.2 | async-start | bytes 524288 | tf_op jit(solution)/shard_map/all_to_all | solution.py:595
  61.5 1.3 %invert.1 = (s32[40,128]{1,0:T(8,128)S(1)}, s32[40,128]{1,0:T(8,128)S(1)}) custom-call(s32[40,128]{1,0:T(8,128)S(1)} %get-tuple-element.26.block_ref, s32[40,128]{1,0:T(8,128)S(1)} %get-tuple-element.27.lane_ref), custom_call_target="tpu_custom_call" | custom-call | tf_op jit(solution)/shard_map/invert/pallas_call | solution.py:616
  62.7 0.6 copy.13
  63.4 9.1 %all-to-all-done.2.message_ref = f32[128,4,128]{2,1,0:T(4,128)S(1)} async-done(((f32[128,4,128]{2,1,0:T(4,128)}), f32[128,4,128]{2,1,0:T(4,128)S(1)}, u32[]{:S(2)}, u32[]{:S(2)}) %all-to-all-start.2) | async-done | bytes 262176 | tf_op jit(solution)/shard_map/all_to_all | solution.py:595
  72.5 0.0 copy-done.1
  72.5 3.4 %pullback.1 = f32[59,5120]{1,0:T(8,128)} custom-call(f32[128,4,128]{2,1,0:T(4,128)S(1)} %all-to-all-done.2.message_ref, s32[40,128]{1,0:T(8,128)S(1)} %get-tuple-element.28.row_ref, s32[40,128]{1,0:T(8,128)S(1)} %get-tuple-element.29.col_ref, f32[59,5120]{1,0:T(8,128)S(1)} %copy-done.1), custom_call_target="tpu_custom_call" | custom-call | tf_op jit(solution)/shard_map/pullback/pallas_call | solution.py:655
  (1 shorter events, 0.0 us)
Async XLA Ops:
  0.6 29.2 %copy-start.5 = (f32[16,3,256]{2,0,1:T(8,128)S(1)}, f32[16,3,256]{2,0,1:T(8,128)}, u32[]{:S(2)}) copy-start(f32[16,3,256]{2,0,1:T(8,128)} %param.11) | copy-start | bytes 147460
  0.6 29.3 %copy-start.4 = (s32[16]{0:T(128)S(1)}, s32[16]{0:T(128)}, u32[]{:S(2)}) copy-start(s32[16]{0:T(128)} %param.10) | copy-start | bytes 196
  0.7 29.3 %copy-start.3 = (s32[16]{0:T(128)S(1)}, s32[16]{0:T(128)}, u32[]{:S(2)}) copy-start(s32[16]{0:T(128)} %param.9) | copy-start | bytes 196
  0.7 29.3 %copy-start.2 = (s32[16,512]{1,0:T(8,128)S(1)}, s32[16,512]{1,0:T(8,128)}, u32[]{:S(2)}) copy-start(s32[16,512]{1,0:T(8,128)} %slots_ref.1) | copy-start | bytes 98308
  2.2 20.8 %all-to-all-start = ((s32[1,128,40]{2,0,1:T(1,128)}), s32[1,128,40]{2,0,1:T(1,128)S(1)}, u32[]{:S(2)}, u32[]{:S(2)}) async-start(s32[1,128,40]{2,0,1:T(1,128)} %copy.11), calls=%async_computation | async-start | bytes 131072 | tf_op jit(solution)/shard_map/all_to_all | solution.py:599
  13.7 1.3 %copy-start = (f32[59,5120]{1,0:T(8,128)S(1)}, f32[59,5120]{1,0:T(8,128)}, u32[]{:S(2)}) copy-start(f32[59,5120]{1,0:T(8,128)} %params_ref.3) | copy-start | bytes 3624964
  15.4 57.1 %copy-start.1 = (f32[59,5120]{1,0:T(8,128)S(1)}, f32[59,5120]{1,0:T(8,128)}, u32[]{:S(2)}) copy-start(f32[59,5120]{1,0:T(8,128)} %params_ref.3) | copy-start | bytes 3624964
  25.2 15.6 %all-to-all-start.1 = ((f32[128,4,128]{2,1,0:T(4,128)}), f32[128,4,128]{2,1,0:T(4,128)S(1)}, u32[]{:S(2)}, u32[]{:S(2)}) async-start(f32[128,4,128]{2,1,0:T(4,128)} %get-tuple-element.18), calls=%async_computation.1 | async-start | bytes 524288 | tf_op jit(solution)/shard_map/all_to_all | solution.py:595
  56.9 15.6 %all-to-all-start.2 = ((f32[128,4,128]{2,1,0:T(4,128)}), f32[128,4,128]{2,1,0:T(4,128)S(1)}, u32[]{:S(2)}, u32[]{:S(2)}) async-start(f32[128,4,128]{2,1,0:T(4,128)} %get-tuple-element.25), calls=%async_computation.2 | async-start | bytes 524288 | tf_op jit(solution)/shard_map/all_to_all | solution.py:595

commit v2 on v1

--- a/solution.py
+++ b/solution.py
@@ -47,6 +47,7 @@
 BACK_UNROLL = 2
 SHORT_UNROLL = 23
 BF16 = jnp.bfloat16
+MESH_ID = pl.DeviceIdType.MESH
 F32 = jnp.float32
 I32 = jnp.int32
 VMEM_LIMIT = 48 * 1024 * 1024
@@ -116,7 +117,7 @@
     return [params_ref[row : row + 1, columns].reshape(8, 128) for row in range(PARAMS)]
 
 
-def project_kernel(params_ref, screen_ref, ninth_ref):
+def project_all(params_ref, screen_ref, ninth_ref):
     def one_group(group, carry):
         screen = project(load_rows(params_ref, group))
         for row in range(8):
@@ -262,29 +263,50 @@
     ninth_ref[...] = last[64 : 64 + CAP].reshape(CAP // 8, 8, 128)
 
 
+def greet(me):
+    barrier = pltpu.get_barrier_semaphore()
+
+    def one(turn, carry):
+        pl.semaphore_signal(
+            barrier, inc=1, device_id=(lax.rem(me + turn, DEVICES),), device_id_type=MESH_ID
+        )
+        return carry
+
+    lax.fori_loop(1, DEVICES, one, 0)
+
+
+def await_greetings():
+    pl.semaphore_wait(pltpu.get_barrier_semaphore(), DEVICES - 1)
+
+
+def send_all(source_ref, landing_ref, send_sem, receive_sem, own_sem, me):
+    def one(turn, carry):
+        peer = lax.rem(me + turn, DEVICES)
+        pltpu.make_async_remote_copy(
+            src_ref=source_ref.at[peer],
+            dst_ref=landing_ref.at[me],
+            send_sem=send_sem,
+            recv_sem=receive_sem,
+            device_id=(peer,),
+            device_id_type=MESH_ID,
+        ).start()
+        return carry
+
+    lax.fori_loop(1, DEVICES, one, 0)
+    pltpu.make_async_copy(source_ref.at[me], landing_ref.at[me], own_sem).start()
+
+
+def await_all(source_ref, landing_ref, send_sem, receive_sem, own_sem, me):
+    others = pl.ds(0, DEVICES - 1)
+    pltpu.make_async_copy(source_ref.at[me], landing_ref.at[me], own_sem).wait()
+    pltpu.make_async_copy(landing_ref.at[others], landing_ref.at[others], receive_sem).wait()
+    pltpu.make_async_copy(source_ref.at[others], source_ref.at[others], send_sem).wait()
+
+
 def wanted_tables(wanted_ref, block_ref, lane_ref):
-    wide = jnp.concatenate(
-        [wanted_ref[...].astype(F32), jnp.zeros((DEVICES, 128 - CAP), F32)], axis=1
-    )
-    wanted = wide.T[0:CAP].astype(I32)
+    wanted = wanted_ref[:, 0, :].astype(F32).T[0:CAP].astype(I32)
     block_ref[...] = wanted >> 7
     lane_ref[...] = wanted & 127
-
-
-def send_kernel(
-    wanted_ref, screen_ref, ninth_ref, message_ref, block_ref, lane_ref,
-    out_ref, out_ninth_ref, split_ref,
-):
-    wanted_tables(wanted_ref, block_ref, lane_ref)
-    gather(
-        screen_ref, ninth_ref, block_ref, lane_ref, out_ref, out_ninth_ref, split_ref,
-        CAP, BLOCKS, 10, 10,
-    )
-    pack_messages(out_ref, out_ninth_ref, message_ref)
-
-
-def invert_kernel(block_ref, lane_ref, row_ref, col_ref, left_ref, right_ref):
-    invert(block_ref, lane_ref, left_ref, right_ref, row_ref, col_ref, CAP, BLOCKS)
 
 
 def lane_map(count_ref, place_ref):
@@ -312,7 +334,7 @@
     return tile, segment, segments, count, origin_x, origin_y
 
 
-def index_kernel(
+def index_tables(
     count_ref, place_ref, slots_ref,
     block_ref, lane_ref, row_ref, col_ref, lanes_ref, all_ref, left_ref, right_ref,
 ):
@@ -346,14 +368,64 @@
     invert(block_ref, lane_ref, left_ref, right_ref, row_ref, col_ref, SEG, CAP)
 
 
+def fetch_kernel(
+    requests_ref, params_ref, count_ref, place_ref, slots_ref,
+    source_ref, source_ninth_ref, block_ref, lane_ref, row_ref, col_ref, lanes_ref,
+    wanted_block_ref, wanted_lane_ref,
+    request_ref, wanted_ref, vmem_params_ref, screen_ref, ninth_ref, out_ref, out_ninth_ref,
+    split_ref, message_ref, landing_ref, all_ref, left_ref, right_ref,
+    params_sem, request_send_sem, request_sem, request_own_sem, send_sem, receive_sem, own_sem,
+):
+    me = lax.axis_index("dev")
+    load = pltpu.make_async_copy(params_ref, vmem_params_ref, params_sem)
+    load.start()
+    greet(me)
+    request_ref[:, 0, :] = jnp.concatenate(
+        [requests_ref[0], jnp.zeros((DEVICES, 128 - CAP), I32)], axis=1
+    )
+    await_greetings()
+    request_sems = (request_send_sem, request_sem, request_own_sem, me)
+    send_all(request_ref, wanted_ref, *request_sems)
+    load.wait()
+    project_all(vmem_params_ref, screen_ref, ninth_ref)
+    index_tables(
+        count_ref, place_ref, slots_ref,
+        block_ref, lane_ref, row_ref, col_ref, lanes_ref, all_ref, left_ref, right_ref,
+    )
+    await_all(request_ref, wanted_ref, *request_sems)
+    wanted_tables(wanted_ref, wanted_block_ref, wanted_lane_ref)
+    gather(
+        screen_ref, ninth_ref, wanted_block_ref, wanted_lane_ref, out_ref, out_ninth_ref,
+        split_ref, CAP, BLOCKS, 10, 10,
+    )
+    pack_messages(out_ref, out_ninth_ref, message_ref)
+    sems = (send_sem, receive_sem, own_sem, me)
+    send_all(message_ref, landing_ref, *sems)
+    await_all(message_ref, landing_ref, *sems)
+    unpack_messages(landing_ref, source_ref, source_ninth_ref)
+
+
+def return_kernel(
+    message_ref, block_ref, lane_ref, source_ref, source_ninth_ref, row_ref, col_ref,
+    landing_ref, left_ref, right_ref, send_sem, receive_sem, own_sem,
+):
+    me = lax.axis_index("dev")
+    greet(me)
+    await_greetings()
+    sems = (send_sem, receive_sem, own_sem, me)
+    send_all(message_ref, landing_ref, *sems)
+    invert(block_ref, lane_ref, left_ref, right_ref, row_ref, col_ref, CAP, BLOCKS)
+    await_all(message_ref, landing_ref, *sems)
+    unpack_messages(landing_ref, source_ref, source_ninth_ref)
+
+
 def render_kernel(
-    message_ref, block_ref, lane_ref, row_ref, col_ref, lanes_ref, target_ref,
+    source_ref, source_ninth_ref, block_ref, lane_ref, row_ref, col_ref, lanes_ref, target_ref,
     rendered_ref, gradient_ref,
-    source_ref, source_ninth_ref, rows_ref, ninth_ref, pre_ref, alpha_ref, weight_ref,
+    rows_ref, ninth_ref, pre_ref, alpha_ref, weight_ref,
     trans_ref, colour_ref, behind_ref, moment_ref, grad_ref, grad_ninth_ref,
     back_ref, back_ninth_ref, split_ref, split_back_ref,
 ):
-    unpack_messages(message_ref, source_ref, source_ninth_ref)
     gather(
         source_ref, source_ninth_ref, block_ref, lane_ref, rows_ref, ninth_ref, split_ref,
         SEG, CAP, 12, 11,
@@ -538,10 +610,9 @@
 
 
 def pullback_kernel(
-    message_ref, row_ref, col_ref, params_ref, gradient_ref,
-    source_ref, source_ninth_ref, rows_ref, ninth_ref, split_ref,
+    source_ref, source_ninth_ref, row_ref, col_ref, params_ref, gradient_ref,
+    rows_ref, ninth_ref, split_ref,
 ):
-    unpack_messages(message_ref, source_ref, source_ninth_ref)
     gather(
         source_ref, source_ninth_ref, row_ref, col_ref, rows_ref, ninth_ref, split_ref,
         BLOCKS, CAP, 10, 10,
@@ -568,17 +639,18 @@
     return jax.ShapeDtypeStruct(dims, dtype)
 
 
-def call(kernel, outs, scratch, name, smem=0, operands=0):
-    params = pltpu.CompilerParams(vmem_limit_bytes=VMEM_LIMIT)
-    specs = [pl.BlockSpec(memory_space=pltpu.SMEM)] * smem
-    specs += [pl.BlockSpec(memory_space=pltpu.VMEM)] * (operands - smem)
+def call(kernel, outs, specs, scratch, name, collective=None):
+    params = {"vmem_limit_bytes": VMEM_LIMIT}
+    if collective is not None:
+        params.update(collective_id=collective, has_side_effects=True)
+    spaces = {"v": pltpu.VMEM, "s": pltpu.SMEM, "h": pl.ANY}
     return pl.pallas_call(
         kernel,
         out_shape=outs,
-        in_specs=specs,
+        in_specs=[pl.BlockSpec(memory_space=spaces[kind]) for kind in specs],
         out_specs=[pl.BlockSpec(memory_space=pltpu.VMEM)] * len(outs),
         scratch_shapes=scratch,
-        compiler_params=params,
+        compiler_params=pltpu.CompilerParams(**params),
         name=name,
     )
 
@@ -586,61 +658,40 @@
 SPLIT = (3 * (CAP // 2 * 8 + 24), 256)
 SPLIT_BACK = (3 * (SEG // 2 * 8 + 24), 256)
 MESSAGE = (DEVICES, 4, 128)
+REQUEST = (DEVICES, 1, 128)
 TABLE = (CAP, 128)
+STEPS = (SEG_PAD, 128)
 EIGHT = (CAP, 8, 128)
 NINE = (CAP // 8, 8, 128)
 
 
-def exchange(messages):
-    return lax.all_to_all(messages, "dev", split_axis=0, concat_axis=0, tiled=True)
-
-
-def exchange_requests(requests):
-    return lax.all_to_all(requests, "dev", split_axis=1, concat_axis=0, tiled=True)
-
-
 def local(params, requests, tile_slots, tile_count, tile_place, target):
     vmem = pltpu.VMEM
-    wanted = exchange_requests(requests).reshape(DEVICES, CAP)
-    screen, ninth = call(
-        project_kernel, [shape(EIGHT), shape(NINE)], [], "project", operands=1
-    )(params)
-    messages, wanted_block, wanted_lane = call(
-        send_kernel,
-        [shape(MESSAGE), shape(TABLE, I32), shape(TABLE, I32)],
-        [vmem(EIGHT, F32), vmem(TABLE, F32), vmem(SPLIT, BF16)],
-        "send",
-        operands=3,
-    )(wanted, screen, ninth)
-    received = exchange(messages)
-    owner_row, owner_col = call(
-        invert_kernel,
-        [shape(TABLE, I32), shape(TABLE, I32)],
-        [vmem((2 * BLOCKS, CAP * 128), BF16), vmem((128, CAP * 128), BF16)],
-        "invert",
-        operands=2,
-    )(wanted_block, wanted_lane)
-    steps = (SEG_PAD, 128)
-    block, lane, slot_row, slot_col, lanes = call(
-        index_kernel,
+    sems = [pltpu.SemaphoreType.DMA] * 3
+    source, source_ninth, block, lane, slot_row, slot_col, lanes, wanted_block, wanted_lane = call(
+        fetch_kernel,
         [
-            shape(steps, I32), shape(steps, I32), shape(TABLE, I32), shape(TABLE, I32),
-            shape((8, 128), I32),
+            shape(EIGHT), shape(NINE), shape(STEPS, I32), shape(STEPS, I32), shape(TABLE, I32),
+            shape(TABLE, I32), shape((8, 128), I32), shape(TABLE, I32), shape(TABLE, I32),
         ],
+        "vhssv",
         [
+            vmem(REQUEST, I32), vmem(REQUEST, I32), vmem((PARAMS, OWNED), F32),
+            vmem(EIGHT, F32), vmem(NINE, F32), vmem(EIGHT, F32), vmem(TABLE, F32),
+            vmem(SPLIT, BF16), vmem(MESSAGE, F32), vmem(MESSAGE, F32),
             vmem((SEGS * SEG + 8, 128), F32),
             vmem((2 * CAP, SEG * 128), BF16), vmem((128, SEG * 128), BF16),
+            pltpu.SemaphoreType.DMA, *sems, *sems,
         ],
-        "index",
-        smem=2,
-        operands=3,
-    )(tile_count.reshape(1, TILES), tile_place.reshape(1, TILES), tile_slots)
+        "fetch",
+        0,
+    )(requests, params, tile_count.reshape(1, TILES), tile_place.reshape(1, TILES), tile_slots)
     rendered, gradients = call(
         render_kernel,
         [shape((TILES, 3, 256)), shape(MESSAGE)],
+        "vvvvvvvv",
         [
-            vmem(EIGHT, F32), vmem(NINE, F32),
-            vmem((SEG, 8, 128), F32), vmem(steps, F32),
+            vmem((SEG, 8, 128), F32), vmem(STEPS, F32),
             vmem((SEG, 12, 8, 128), F32),
             vmem((PASSES, SEG, GROUP, 8, 128), F32), vmem((PASSES, SEG, GROUP, 8, 128), F32),
             vmem((256, 128), F32), vmem((3, 256, 128), F32), vmem((256, 128), F32),
@@ -649,19 +700,26 @@
             vmem(EIGHT, F32), vmem(TABLE, F32), vmem(SPLIT, BF16), vmem(SPLIT_BACK, BF16),
         ],
         "render",
-        operands=7,
-    )(received, block, lane, slot_row, slot_col, lanes, target)
-    returned = exchange(gradients)
+    )(source, source_ninth, block, lane, slot_row, slot_col, lanes, target)
+    back, back_ninth, owner_row, owner_col = call(
+        return_kernel,
+        [shape(EIGHT), shape(NINE), shape(TABLE, I32), shape(TABLE, I32)],
+        "vvv",
+        [
+            vmem(MESSAGE, F32),
+            vmem((2 * BLOCKS, CAP * 128), BF16), vmem((128, CAP * 128), BF16),
+            *sems,
+        ],
+        "return",
+        1,
+    )(gradients, wanted_block, wanted_lane)
     (gradient,) = call(
         pullback_kernel,
         [shape((PARAMS, OWNED))],
-        [
-            vmem(EIGHT, F32), vmem(NINE, F32), vmem(EIGHT, F32), vmem(TABLE, F32),
-            vmem(SPLIT, BF16),
-        ],
+        "vvvvv",
+        [vmem(EIGHT, F32), vmem(TABLE, F32), vmem(SPLIT, BF16)],
         "pullback",
-        operands=4,
-    )(returned, owner_row, owner_col, params)
+    )(back, back_ninth, owner_row, owner_col, params)
     return rendered, gradient
 
 

time: 76.2 us -> 64.4 us (0.85)
  Pallas kernels: 25.7 us -> 57.7 us
  waiting for transfers between devices: 25.3 us -> 0 us
  starting transfers between devices: 20.6 us -> 0 us
  local copies, waits for them, and re-layouts: 3.5 us -> 5.67 us
    pallas_call x6 -> x4, Pallas kernels: 25.7 us -> 57.7 us  [the longest x1 26.5 us: local(): call(fetch_kernel, [shape(EIGHT), shape(NINE), shape(STEPS, I32), shape(S...]
    all_to_all x3 -> x0, waiting for transfers between devices: 25.3 us -> none  [the longest x2 17.7 us: exchange(): lax.all_to_all(messages, 'dev', split_axis=0, concat_axis=0, tiled=True)]
    all_to_all x3 -> x0, starting transfers between devices: 20.6 us -> none  [the longest x1 11.5 us: exchange_requests(): lax.all_to_all(requests, 'dev', split_axis=1, concat_axis=0, tiled=True)]
    unnamed x15 -> x13, local copies, waits for them, and re-layouts: 3.5 us -> 5.67 us
  transfers between devices with their start and end apart: 3 -> 0, of which waited for: 3 -> 0; matrix products, arithmetic and copies ran while one was open for 1% -> 0% of each run, Pallas kernels for 5% -> 0%
where the time goes in v2:
time: 64.4 us; the launch traced here: 64.1 us
  Pallas kernels  57.7 us (90%)
  local copies, waits for them, and re-layouts  5.67 us (9%)
  between operations  0.68 us (1%)
    pallas_call x1, Pallas kernels, local(): call(fetch_kernel, [shape(EIGHT), shape(NINE), shape(STEPS, I32), shape(S...  26.5 us
    pallas_call x1, Pallas kernels, local(): call(render_kernel, [shape((TILES, 3, 256)), shape(MESSAGE)], 'vvvvvvvv',...  15.2 us
    pallas_call x1, Pallas kernels, local(): call(return_kernel, [shape(EIGHT), shape(NINE), shape(TABLE, I32), shape(...  12.6 us
    unnamed x13, local copies, waits for them, and re-layouts  5.67 us
    pallas_call x1, Pallas kernels, local(): call(pullback_kernel, [shape((PARAMS, OWNED))], 'vvvvv', [vmem(EIGHT, F32...  3.33 us

profile of v2, /device:TPU:1, one launch (start us, length us, event | category | flops | bytes accessed | tf_op | source)
XLA Modules:
  0.0 64.1 jit_solution(14332651778766735)
XLA Ops:
  0.6 0.8 %copy.8.requests_ref = s32[1,128,40]{2,1,0:T(8,128)S(1)} copy(s32[1,128,40]{1,2,0:T(8,128)} %param.7) | data formatting | bytes 40960 | tf_op args[1]
  1.5 0.8 %copy.9.target_ref = f32[16,3,256]{2,1,0:T(4,128)S(1)} copy(f32[16,3,256]{2,0,1:T(8,128)} %param.11) | data formatting | bytes 98304 | tf_op args[5]
  2.3 0.0 copy-start
  2.3 1.3 %copy-done = f32[59,5120]{1,0:T(8,128)S(1)} copy-done((f32[59,5120]{1,0:T(8,128)S(1)}, f32[59,5120]{1,0:T(8,128)}, u32[]{:S(2)}) %copy-start) | copy-done | bytes 1208344
  3.6 0.0 copy-start.2
  3.6 0.8 %copy-done.2 = s32[16,512]{1,0:T(8,128)S(1)} copy-done((s32[16,512]{1,0:T(8,128)S(1)}, s32[16,512]{1,0:T(8,128)}, u32[]{:S(2)}) %copy-start.2) | copy-done | bytes 32792
  4.4 0.0 copy-start.3
  4.4 0.7 %copy-done.3 = s32[16]{0:T(128)S(1)} copy-done((s32[16]{0:T(128)S(1)}, s32[16]{0:T(128)}, u32[]{:S(2)}) %copy-start.3) | copy-done | bytes 88
  5.0 0.0 copy-start.4
  5.0 0.7 %copy-done.4 = s32[16]{0:T(128)S(1)} copy-done((s32[16]{0:T(128)S(1)}, s32[16]{0:T(128)}, u32[]{:S(2)}) %copy-start.4) | copy-done | bytes 88
  5.7 0.0 copy-start.1
  5.7 26.5 %fetch.1 = (f32[40,8,128]{2,1,0:T(8,128)S(1)}, f32[5,8,128]{2,1,0:T(8,128)S(1)}, s32[48,128]{1,0:T(8,128)S(1)}, s32[48,128]{1,0:T(8,128)S(1)}, s32[40,128]{1,0:T...) custom-call(s32[1,128,40]{2,1,0:T(8,128)S(1)} %copy.8.requests_ref, ...), custom_call_target="tpu_custom_call" | custom-call | tf_op jit(solution)/shard_map/fetch/pallas_call | solution.py:671
  32.2 15.2 %render.1 = (f32[16,3,256]{2,1,0:T(4,128)S(1)}, f32[128,4,128]{2,1,0:T(4,128)S(1)}) custom-call(f32[40,8,128]{2,1,0:T(8,128)S(1)} %get-tuple-element.17.source_ref, f32[5,8,128]{2,1,0:T(8,128)S(1)} %get-tuple-element.18.source_ninth_ref, s32[48,128]{1,0:T(8,128)S(1)} %get-tuple-element.19.block_ref, s32[48,128]{1,0:T(8,128)S(1)} %get-tuple-element.20.lane_ref, ...), custom_call_target="tpu_custom_call" | custom-call | tf_op jit(solution)/shard_map/render/pallas_call | solution.py:689
  47.4 0.6 copy.10
  48.1 12.6 %return.1 = (f32[40,8,128]{2,1,0:T(8,128)S(1)}, f32[5,8,128]{2,1,0:T(8,128)S(1)}, s32[40,128]{1,0:T(8,128)S(1)}, s32[40,128]{1,0:T(8,128)S(1)}) custom-call(f32[128,4,128]{2,1,0:T(4,128)S(1)} %get-tuple-element.25.message_ref, s32[40,128]{1,0:T(8,128)S(1)} %get-tuple-element.26.block_ref, s32[40,128]{1,0:T(8,128)S(1)} %get-tuple-element.27.lane_ref), custom_call_target="tpu_custom_call" | custom-call | tf_op jit(solution)/shard_map/return/pallas_call | solution.py:704
  60.7 0.0 copy-done.1
  60.7 3.3 %pullback.1 = f32[59,5120]{1,0:T(8,128)} custom-call(f32[40,8,128]{2,1,0:T(8,128)S(1)} %get-tuple-element.28.source_ref, f32[5,8,128]{2,1,0:T(8,128)S(1)} %get-tuple-element.29.source_ninth_ref, s32[40,128]{1,0:T(8,128)S(1)} %get-tuple-element.30.row_ref, s32[40,128]{1,0:T(8,128)S(1)} %get-tuple-element.31.col_ref, f32[59,5120]{1,0:T(8,128)S(1)} %copy-done.1), custom_call_target="tpu_custom_call" | custom-call | tf_op jit(solution)/shard_map/pullback/pallas_call | solution.py:716
Async XLA Ops:
  2.3 1.3 %copy-start = (f32[59,5120]{1,0:T(8,128)S(1)}, f32[59,5120]{1,0:T(8,128)}, u32[]{:S(2)}) copy-start(f32[59,5120]{1,0:T(8,128)} %params_ref.3) | copy-start | bytes 3624964
  3.6 0.8 %copy-start.2 = (s32[16,512]{1,0:T(8,128)S(1)}, s32[16,512]{1,0:T(8,128)}, u32[]{:S(2)}) copy-start(s32[16,512]{1,0:T(8,128)} %slots_ref.1) | copy-start | bytes 98308
  4.4 0.7 %copy-start.3 = (s32[16]{0:T(128)S(1)}, s32[16]{0:T(128)}, u32[]{:S(2)}) copy-start(s32[16]{0:T(128)} %param.9) | copy-start | bytes 196
  5.0 0.7 %copy-start.4 = (s32[16]{0:T(128)S(1)}, s32[16]{0:T(128)}, u32[]{:S(2)}) copy-start(s32[16]{0:T(128)} %param.10) | copy-start | bytes 196
  5.7 55.1 %copy-start.1 = (f32[59,5120]{1,0:T(8,128)S(1)}, f32[59,5120]{1,0:T(8,128)}, u32[]{:S(2)}) copy-start(f32[59,5120]{1,0:T(8,128)} %params_ref.3) | copy-start | bytes 3624964

commit v3 on v2

--- a/solution.py
+++ b/solution.py
@@ -50,7 +50,7 @@
 MESH_ID = pl.DeviceIdType.MESH
 F32 = jnp.float32
 I32 = jnp.int32
-VMEM_LIMIT = 48 * 1024 * 1024
+VMEM_LIMIT = 64 * 1000 * 1000
 
 
 def project(rows):
@@ -112,14 +112,15 @@
     ]
 
 
-def load_rows(params_ref, group):
-    columns = pl.ds(pl.multiple_of(group * 1024, 1024), 1024)
+def load_rows(params_ref, columns):
     return [params_ref[row : row + 1, columns].reshape(8, 128) for row in range(PARAMS)]
 
 
 def project_all(params_ref, screen_ref, ninth_ref):
     def one_group(group, carry):
-        screen = project(load_rows(params_ref, group))
+        screen = project(
+            load_rows(params_ref, pl.ds(pl.multiple_of(group * 1024, 1024), 1024))
+        )
         for row in range(8):
             screen_ref[pl.ds(pl.multiple_of(group * 8, 8), 8), row, :] = screen[row]
         ninth_ref[group] = screen[8]
@@ -252,7 +253,6 @@
         [flat[256:320], ninth_ref[...], jnp.zeros((128 - 64 - CAP, 128), F32)], axis=0
     )
     out_ref[:, 2, :] = last.T
-    out_ref[:, 3, :] = jnp.zeros((128, 128), F32)
 
 
 def unpack_messages(message_ref, rows_ref, ninth_ref):
@@ -319,8 +319,8 @@
     origin_y = jnp.zeros((1, 128), I32)
     base = jnp.int32(0)
     for index in range(TILES):
-        listed = count_ref[0, index]
-        place = place_ref[0, index]
+        listed = count_ref[index]
+        place = place_ref[index]
         used = lax.div(listed + (SEG - 1), SEG)
         inside = (lane >= base) & (lane < base + used)
         place_y = lax.div(place, 120)
@@ -368,58 +368,7 @@
     invert(block_ref, lane_ref, left_ref, right_ref, row_ref, col_ref, SEG, CAP)
 
 
-def fetch_kernel(
-    requests_ref, params_ref, count_ref, place_ref, slots_ref,
-    source_ref, source_ninth_ref, block_ref, lane_ref, row_ref, col_ref, lanes_ref,
-    wanted_block_ref, wanted_lane_ref,
-    request_ref, wanted_ref, vmem_params_ref, screen_ref, ninth_ref, out_ref, out_ninth_ref,
-    split_ref, message_ref, landing_ref, all_ref, left_ref, right_ref,
-    params_sem, request_send_sem, request_sem, request_own_sem, send_sem, receive_sem, own_sem,
-):
-    me = lax.axis_index("dev")
-    load = pltpu.make_async_copy(params_ref, vmem_params_ref, params_sem)
-    load.start()
-    greet(me)
-    request_ref[:, 0, :] = jnp.concatenate(
-        [requests_ref[0], jnp.zeros((DEVICES, 128 - CAP), I32)], axis=1
-    )
-    await_greetings()
-    request_sems = (request_send_sem, request_sem, request_own_sem, me)
-    send_all(request_ref, wanted_ref, *request_sems)
-    load.wait()
-    project_all(vmem_params_ref, screen_ref, ninth_ref)
-    index_tables(
-        count_ref, place_ref, slots_ref,
-        block_ref, lane_ref, row_ref, col_ref, lanes_ref, all_ref, left_ref, right_ref,
-    )
-    await_all(request_ref, wanted_ref, *request_sems)
-    wanted_tables(wanted_ref, wanted_block_ref, wanted_lane_ref)
-    gather(
-        screen_ref, ninth_ref, wanted_block_ref, wanted_lane_ref, out_ref, out_ninth_ref,
-        split_ref, CAP, BLOCKS, 10, 10,
-    )
-    pack_messages(out_ref, out_ninth_ref, message_ref)
-    sems = (send_sem, receive_sem, own_sem, me)
-    send_all(message_ref, landing_ref, *sems)
-    await_all(message_ref, landing_ref, *sems)
-    unpack_messages(landing_ref, source_ref, source_ninth_ref)
-
-
-def return_kernel(
-    message_ref, block_ref, lane_ref, source_ref, source_ninth_ref, row_ref, col_ref,
-    landing_ref, left_ref, right_ref, send_sem, receive_sem, own_sem,
-):
-    me = lax.axis_index("dev")
-    greet(me)
-    await_greetings()
-    sems = (send_sem, receive_sem, own_sem, me)
-    send_all(message_ref, landing_ref, *sems)
-    invert(block_ref, lane_ref, left_ref, right_ref, row_ref, col_ref, CAP, BLOCKS)
-    await_all(message_ref, landing_ref, *sems)
-    unpack_messages(landing_ref, source_ref, source_ninth_ref)
-
-
-def render_kernel(
+def render(
     source_ref, source_ninth_ref, block_ref, lane_ref, row_ref, col_ref, lanes_ref, target_ref,
     rendered_ref, gradient_ref,
     rows_ref, ninth_ref, pre_ref, alpha_ref, weight_ref,
@@ -504,8 +453,8 @@
             pick, colour_ref[channel] * start, (((1,), (1,)), ((), ())),
             preferred_element_type=F32, precision=lax.Precision.HIGHEST,
         )
-        rendered_ref[:, channel, :] = image
-        error = (image - target_ref[:, channel, :]) * (1.0 / 256.0)
+        rendered_ref[channel] = image
+        error = (image - target_ref[channel]) * (1.0 / 256.0)
         spread = lax.dot_general(
             error, pick, (((0,), (0,)), ((), ())),
             preferred_element_type=F32, precision=lax.Precision.HIGHEST,
@@ -609,19 +558,128 @@
     pack_messages(back_ref, back_ninth_ref, gradient_ref)
 
 
+def step_kernel(
+    requests_ref, params_ref, count_ref, place_ref, slots_ref, target_ref,
+    far_rendered_ref, far_back_ref, far_back_ninth_ref, far_owner_row_ref, far_owner_col_ref,
+    rendered_ref, back_ref, back_ninth_ref, owner_row_ref, owner_col_ref, store_sem,
+    here_requests_ref, here_params_ref, here_count_ref, here_place_ref, here_slots_ref,
+    here_target_ref, load_sem,
+    request_ref, wanted_ref, wanted_block_ref, wanted_lane_ref, request_send, request_receive,
+    request_own,
+    screen_ref, ninth_ref, out_ref, out_ninth_ref, split_ref, left_ref, right_ref,
+    all_ref, slot_left_ref, slot_right_ref, block_ref, lane_ref, row_ref, col_ref, lanes_ref,
+    message_ref, landing_ref, send_sem, receive_sem, own_sem, source_ref, source_ninth_ref,
+    reply_ref, reply_landing_ref, reply_send, reply_receive, reply_own,
+    *render_refs,
+):
+    me = lax.axis_index("dev")
+    loads = [
+        pltpu.make_async_copy(far, near, load_sem.at[index])
+        for index, (far, near) in enumerate(
+            (
+                (requests_ref, here_requests_ref),
+                (params_ref, here_params_ref),
+                (count_ref, here_count_ref),
+                (place_ref, here_place_ref),
+                (slots_ref, here_slots_ref),
+                (target_ref, here_target_ref),
+            )
+        )
+    ]
+    for load in loads:
+        load.start()
+    greet(me)
+    loads[0].wait()
+    wide = jnp.concatenate(
+        [here_requests_ref[...].astype(F32), jnp.zeros((128 - CAP, DEVICES), F32)], axis=0
+    )
+    request_ref[:, 0, :] = wide.T.astype(I32)
+    await_greetings()
+    request_sems = (request_send, request_receive, request_own, me)
+    send_all(request_ref, wanted_ref, *request_sems)
+    for load in loads[1:]:
+        load.wait()
+    project_all(here_params_ref, screen_ref, ninth_ref)
+    index_tables(
+        here_count_ref, here_place_ref, here_slots_ref,
+        block_ref, lane_ref, row_ref, col_ref, lanes_ref, all_ref, slot_left_ref, slot_right_ref,
+    )
+    await_all(request_ref, wanted_ref, *request_sems)
+    wanted_tables(wanted_ref, wanted_block_ref, wanted_lane_ref)
+    gather(
+        screen_ref, ninth_ref, wanted_block_ref, wanted_lane_ref, out_ref, out_ninth_ref,
+        split_ref, CAP, BLOCKS, 10, 10,
+    )
+    pack_messages(out_ref, out_ninth_ref, message_ref)
+    sems = (send_sem, receive_sem, own_sem, me)
+    send_all(message_ref, landing_ref, *sems)
+    invert(
+        wanted_block_ref, wanted_lane_ref, left_ref, right_ref, owner_row_ref, owner_col_ref,
+        CAP, BLOCKS,
+    )
+    await_all(message_ref, landing_ref, *sems)
+    unpack_messages(landing_ref, source_ref, source_ninth_ref)
+    render(
+        source_ref, source_ninth_ref, block_ref, lane_ref, row_ref, col_ref, lanes_ref,
+        here_target_ref, rendered_ref, reply_ref, *render_refs,
+    )
+    reply_sems = (reply_send, reply_receive, reply_own, me)
+    send_all(reply_ref, reply_landing_ref, *reply_sems)
+    stores = [
+        pltpu.make_async_copy(near, far, store_sem.at[index])
+        for index, (near, far) in enumerate(
+            (
+                (rendered_ref, far_rendered_ref),
+                (owner_row_ref, far_owner_row_ref),
+                (owner_col_ref, far_owner_col_ref),
+                (back_ref, far_back_ref),
+                (back_ninth_ref, far_back_ninth_ref),
+            )
+        )
+    ]
+    for store in stores[:3]:
+        store.start()
+    await_all(reply_ref, reply_landing_ref, *reply_sems)
+    unpack_messages(reply_landing_ref, back_ref, back_ninth_ref)
+    for store in stores[3:]:
+        store.start()
+    for store in stores:
+        store.wait()
+
+
 def pullback_kernel(
-    source_ref, source_ninth_ref, row_ref, col_ref, params_ref, gradient_ref,
-    rows_ref, ninth_ref, split_ref,
+    far_source_ref, far_ninth_ref, far_row_ref, far_col_ref, image_ref, params_ref,
+    rendered_ref, gradient_ref,
+    source_ref, source_ninth_ref, row_ref, col_ref,
+    rows_ref, ninth_ref, split_ref, here_params_ref, here_gradient_ref, load_sem, store_sem,
 ):
+    loads = [
+        pltpu.make_async_copy(far, near, load_sem.at[index])
+        for index, (far, near) in enumerate(
+            (
+                (far_source_ref, source_ref),
+                (far_ninth_ref, source_ninth_ref),
+                (far_row_ref, row_ref),
+                (far_col_ref, col_ref),
+                (params_ref, here_params_ref),
+                (image_ref, rendered_ref),
+            )
+        )
+    ]
+    for load in loads:
+        load.start()
+    for load in loads[:4]:
+        load.wait()
     gather(
         source_ref, source_ninth_ref, row_ref, col_ref, rows_ref, ninth_ref, split_ref,
         BLOCKS, CAP, 10, 10,
     )
-
-    def one_group(group, carry):
-        columns = pl.ds(pl.multiple_of(group * 1024, 1024), 1024)
-        eight = pl.ds(pl.multiple_of(group * 8, 8), 8)
-        rows = load_rows(params_ref, group)
+    loads[4].wait()
+    stores = []
+    for group in range(OWNED // 1024):
+        columns = pl.ds(group * 1024, 1024)
+        eight = pl.ds(group * 8, 8)
+        rows = load_rows(here_params_ref, columns)
         screen_grad = [rows_ref[eight, row, :] for row in range(8)] + [ninth_ref[eight, :]]
         screen, pullback = jax.vjp(project, rows)
         by_logit = screen_grad[5] * (1.0 / (1.0 + jnp.exp(rows[10])))
@@ -629,26 +687,32 @@
         (grads,) = pullback(screen_grad)
         grads[10] = by_logit
         for row in range(PARAMS):
-            gradient_ref[row : row + 1, columns] = grads[row].reshape(1, 1024)
-        return carry
-
-    lax.fori_loop(0, OWNED // 1024, one_group, 0)
+            here_gradient_ref[row : row + 1, columns] = grads[row].reshape(1, 1024)
+        stores.append(
+            pltpu.make_async_copy(
+                here_gradient_ref.at[:, columns], gradient_ref.at[:, columns], store_sem.at[group]
+            )
+        )
+        stores[-1].start()
+    for store in stores:
+        store.wait()
+    loads[5].wait()
 
 
 def shape(dims, dtype=F32):
     return jax.ShapeDtypeStruct(dims, dtype)
 
 
-def call(kernel, outs, specs, scratch, name, collective=None):
+def call(kernel, outs, specs, out_specs, scratch, name, collective=None):
     params = {"vmem_limit_bytes": VMEM_LIMIT}
     if collective is not None:
         params.update(collective_id=collective, has_side_effects=True)
-    spaces = {"v": pltpu.VMEM, "s": pltpu.SMEM, "h": pl.ANY}
+    spaces = {"v": pltpu.VMEM, "s": pltpu.SMEM, "h": pltpu.HBM}
     return pl.pallas_call(
         kernel,
         out_shape=outs,
         in_specs=[pl.BlockSpec(memory_space=spaces[kind]) for kind in specs],
-        out_specs=[pl.BlockSpec(memory_space=pltpu.VMEM)] * len(outs),
+        out_specs=[pl.BlockSpec(memory_space=spaces[kind]) for kind in out_specs],
         scratch_shapes=scratch,
         compiler_params=pltpu.CompilerParams(**params),
         name=name,
@@ -657,7 +721,7 @@
 
 SPLIT = (3 * (CAP // 2 * 8 + 24), 256)
 SPLIT_BACK = (3 * (SEG // 2 * 8 + 24), 256)
-MESSAGE = (DEVICES, 4, 128)
+MESSAGE = (DEVICES, 3, 128)
 REQUEST = (DEVICES, 1, 128)
 TABLE = (CAP, 128)
 STEPS = (SEG_PAD, 128)
@@ -665,32 +729,33 @@
 NINE = (CAP // 8, 8, 128)
 
 
+IMAGE = (3, TILES, 256)
+
+
 def local(params, requests, tile_slots, tile_count, tile_place, target):
     vmem = pltpu.VMEM
     sems = [pltpu.SemaphoreType.DMA] * 3
-    source, source_ninth, block, lane, slot_row, slot_col, lanes, wanted_block, wanted_lane = call(
-        fetch_kernel,
+    image, back, back_ninth, owner_row, owner_col = call(
+        step_kernel,
+        [shape(IMAGE), shape(EIGHT), shape(NINE), shape(TABLE, I32), shape(TABLE, I32)],
+        "hhhhhh",
+        "hhhhh",
         [
-            shape(EIGHT), shape(NINE), shape(STEPS, I32), shape(STEPS, I32), shape(TABLE, I32),
-            shape(TABLE, I32), shape((8, 128), I32), shape(TABLE, I32), shape(TABLE, I32),
-        ],
-        "vhssv",
-        [
-            vmem(REQUEST, I32), vmem(REQUEST, I32), vmem((PARAMS, OWNED), F32),
+            vmem(IMAGE, F32), vmem(EIGHT, F32), vmem(NINE, F32), vmem(TABLE, I32),
+            vmem(TABLE, I32), pltpu.SemaphoreType.DMA((5,)),
+            vmem((CAP, DEVICES), I32), vmem((PARAMS, OWNED), F32),
+            pltpu.SMEM((TILES,), I32), pltpu.SMEM((TILES,), I32), vmem((TILES, SLOTS), I32),
+            vmem(IMAGE, F32), pltpu.SemaphoreType.DMA((6,)),
+            vmem(REQUEST, I32), vmem(REQUEST, I32), vmem(TABLE, I32), vmem(TABLE, I32), *sems,
             vmem(EIGHT, F32), vmem(NINE, F32), vmem(EIGHT, F32), vmem(TABLE, F32),
-            vmem(SPLIT, BF16), vmem(MESSAGE, F32), vmem(MESSAGE, F32),
+            vmem(SPLIT, BF16),
+            vmem((2 * BLOCKS, CAP * 128), BF16), vmem((128, CAP * 128), BF16),
             vmem((SEGS * SEG + 8, 128), F32),
             vmem((2 * CAP, SEG * 128), BF16), vmem((128, SEG * 128), BF16),
-            pltpu.SemaphoreType.DMA, *sems, *sems,
-        ],
-        "fetch",
-        0,
-    )(requests, params, tile_count.reshape(1, TILES), tile_place.reshape(1, TILES), tile_slots)
-    rendered, gradients = call(
-        render_kernel,
-        [shape((TILES, 3, 256)), shape(MESSAGE)],
-        "vvvvvvvv",
-        [
+            vmem(STEPS, I32), vmem(STEPS, I32), vmem(TABLE, I32), vmem(TABLE, I32),
+            vmem((8, 128), I32),
+            vmem(MESSAGE, F32), vmem(MESSAGE, F32), *sems, vmem(EIGHT, F32), vmem(NINE, F32),
+            vmem(MESSAGE, F32), vmem(MESSAGE, F32), *sems,
             vmem((SEG, 8, 128), F32), vmem(STEPS, F32),
             vmem((SEG, 12, 8, 128), F32),
             vmem((PASSES, SEG, GROUP, 8, 128), F32), vmem((PASSES, SEG, GROUP, 8, 128), F32),
@@ -699,28 +764,26 @@
             vmem((SEG, 8, 128), F32), vmem((SEG_PAD // 8, 8, 128), F32),
             vmem(EIGHT, F32), vmem(TABLE, F32), vmem(SPLIT, BF16), vmem(SPLIT_BACK, BF16),
         ],
-        "render",
-    )(source, source_ninth, block, lane, slot_row, slot_col, lanes, target)
-    back, back_ninth, owner_row, owner_col = call(
-        return_kernel,
-        [shape(EIGHT), shape(NINE), shape(TABLE, I32), shape(TABLE, I32)],
-        "vvv",
+        "step",
+        0,
+    )(
+        requests.reshape(DEVICES, CAP).T, params, tile_count, tile_place, tile_slots,
+        target.transpose(1, 0, 2),
+    )
+    rendered, gradient = call(
+        pullback_kernel,
+        [shape(IMAGE), shape((PARAMS, OWNED))],
+        "hhhhhh",
+        "hh",
         [
-            vmem(MESSAGE, F32),
-            vmem((2 * BLOCKS, CAP * 128), BF16), vmem((128, CAP * 128), BF16),
-            *sems,
+            vmem(EIGHT, F32), vmem(NINE, F32), vmem(TABLE, I32), vmem(TABLE, I32),
+            vmem(EIGHT, F32), vmem(TABLE, F32), vmem(SPLIT, BF16), vmem((PARAMS, OWNED), F32),
+            vmem((PARAMS, OWNED), F32), pltpu.SemaphoreType.DMA((6,)),
+            pltpu.SemaphoreType.DMA((OWNED // 1024,)),
         ],
-        "return",
-        1,
-    )(gradients, wanted_block, wanted_lane)
-    (gradient,) = call(
-        pullback_kernel,
-        [shape((PARAMS, OWNED))],
-        "vvvvv",
-        [vmem(EIGHT, F32), vmem(TABLE, F32), vmem(SPLIT, BF16)],
         "pullback",
-    )(back, back_ninth, owner_row, owner_col, params)
-    return rendered, gradient
+    )(back, back_ninth, owner_row, owner_col, image, params)
+    return rendered.transpose(1, 0, 2), gradient
 
 
 def solution(mesh):

time: 64.4 us -> 53.1 us (0.82)
  local copies, waits for them, and re-layouts: 5.67 us -> 0 us
  Pallas kernels: 57.7 us -> 52.3 us
    unnamed x13 -> x0, local copies, waits for them, and re-layouts: 5.67 us -> none
    pallas_call x4 -> x2, Pallas kernels: 57.7 us -> 52.3 us  [the longest x1 48.4 us: local(): call(step_kernel, [shape(IMAGE), shape(EIGHT), shape(NINE), shape(TABLE,...]
where the time goes in v3:
time: 53.1 us; the launch traced here: 53 us
  Pallas kernels  52.3 us (98%)
  between operations  0.64 us (1%)
    pallas_call x1, Pallas kernels, local(): call(step_kernel, [shape(IMAGE), shape(EIGHT), shape(NINE), shape(TABLE,...  48.4 us
    pallas_call x1, Pallas kernels, local(): call(pullback_kernel, [shape(IMAGE), shape((PARAMS, OWNED))], 'hhhhhh', '...  3.92 us

profile of v3, /device:TPU:1, one launch (start us, length us, event | category | flops | bytes accessed | tf_op | source)
XLA Modules:
  0.0 53.0 jit_solution(17824570648889437423)
XLA Ops:
  0.6 48.4 %step.1 = (f32[3,16,256]{2,1,0:T(8,128)}, f32[40,8,128]{2,1,0:T(8,128)}, f32[5,8,128]{2,1,0:T(8,128)}, s32[40,128]{1,0:T(8,128)}, s32[40,128]{1,0:T(8,128)}) custom-call(s32[40,128]{1,0:T(8,128)} %bitcast.6, f32[59,5120]{1,0:T(8,128)} %params_ref.3, s32[16]{0:T(128)} %count_ref.1, s32[16]{0:T(128)} %place_ref.1, s32[16,512]{1,0:T(8,128)} %slots_ref.1, ...), custom_call_target="tpu_custom_call" | custom-call | tf_op jit(solution)/shard_map/step/pallas_call | solution.py:738
  49.0 3.9 %pullback.1 = (f32[3,16,256]{2,1,0:T(8,128)}, f32[59,5120]{1,0:T(8,128)}) custom-call(f32[40,8,128]{2,1,0:T(8,128)} %get-tuple-element.9.far_source_ref, f32[5,8,128]{2,1,0:T(8,128)} %get-tuple-element.10.far_ninth_ref, s32[40,128]{1,0:T(8,128)} %get-tuple-element.11.far_row_ref, s32[40,128]{1,0:T(8,128)} %get-tuple-element.12.far_col_ref, ...), custom_call_target="tpu_custom_call" | custom-call | tf_op jit(solution)/shard_map/pullback/pallas_call | solution.py:773

commit v4 on v3

--- a/solution.py
+++ b/solution.py
@@ -32,6 +32,8 @@
 LOG2_E = 1.4426950408889634
 
 DEVICES = 128
+INNER = 8
+OUTER = DEVICES // INNER
 OWNED = 5120
 CAP = 40
 PARAMS = 59
@@ -43,7 +45,7 @@
 SEGS = 12
 GROUP = 8
 PASSES = 32 // GROUP
-STEP_UNROLL = 2
+STEP_UNROLL = 23
 BACK_UNROLL = 2
 SHORT_UNROLL = 23
 BF16 = jnp.bfloat16
@@ -263,20 +265,66 @@
     ninth_ref[...] = last[64 : 64 + CAP].reshape(CAP // 8, 8, 128)
 
 
+def request_peers(me):
+    outer, inner = lax.div(me, INNER), lax.rem(me, INNER)
+    near = [outer * INNER + lax.rem(inner + turn, INNER) for turn in range(1, INNER)]
+    far = [lax.rem(outer + turn, OUTER) * INNER + inner for turn in range(1, OUTER)]
+    return outer, inner, near, far
+
+
 def greet(me):
     barrier = pltpu.get_barrier_semaphore()
-
-    def one(turn, carry):
-        pl.semaphore_signal(
-            barrier, inc=1, device_id=(lax.rem(me + turn, DEVICES),), device_id_type=MESH_ID
-        )
-        return carry
-
-    lax.fori_loop(1, DEVICES, one, 0)
+    _, _, near, far = request_peers(me)
+    for peer in near + far:
+        pl.semaphore_signal(barrier, inc=1, device_id=(peer,), device_id_type=MESH_ID)
 
 
 def await_greetings():
-    pl.semaphore_wait(pltpu.get_barrier_semaphore(), DEVICES - 1)
+    pl.semaphore_wait(pltpu.get_barrier_semaphore(), INNER + OUTER - 2)
+
+
+def send_requests(request_ref, middle_ref, sems, me):
+    send_sem, receive_sem, own_sem = sems
+    _, inner, near, _ = request_peers(me)
+    for peer in near:
+        pltpu.make_async_remote_copy(
+            src_ref=request_ref.at[lax.rem(peer, INNER)],
+            dst_ref=middle_ref.at[inner],
+            send_sem=send_sem,
+            recv_sem=receive_sem,
+            device_id=(peer,),
+            device_id_type=MESH_ID,
+        ).start()
+    pltpu.make_async_copy(request_ref.at[inner], middle_ref.at[inner], own_sem).start()
+
+
+def forward_requests(request_ref, middle_ref, wanted_ref, first_sems, sems, me):
+    first_send, first_receive, first_own = first_sems
+    send_sem, receive_sem, own_sem = sems
+    outer, inner, _, far = request_peers(me)
+    others = pl.ds(0, INNER - 1)
+    pltpu.make_async_copy(request_ref.at[inner], middle_ref.at[inner], first_own).wait()
+    pltpu.make_async_copy(middle_ref.at[others], middle_ref.at[others], first_receive).wait()
+    for peer in far:
+        pltpu.make_async_remote_copy(
+            src_ref=middle_ref.at[:, lax.div(peer, INNER)],
+            dst_ref=wanted_ref.at[outer],
+            send_sem=send_sem,
+            recv_sem=receive_sem,
+            device_id=(peer,),
+            device_id_type=MESH_ID,
+        ).start()
+    pltpu.make_async_copy(middle_ref.at[:, outer], wanted_ref.at[outer], own_sem).start()
+    pltpu.make_async_copy(request_ref.at[others], request_ref.at[others], first_send).wait()
+
+
+def await_requests(middle_ref, wanted_ref, sems, me):
+    send_sem, receive_sem, own_sem = sems
+    outer = lax.div(me, INNER)
+    others = pl.ds(0, OUTER - 1)
+    pltpu.make_async_copy(middle_ref.at[:, outer], wanted_ref.at[outer], own_sem).wait()
+    pltpu.make_async_copy(wanted_ref.at[others], wanted_ref.at[others], receive_sem).wait()
+    pltpu.make_async_copy(wanted_ref.at[others], wanted_ref.at[others], send_sem).wait()
 
 
 def send_all(source_ref, landing_ref, send_sem, receive_sem, own_sem, me):
@@ -304,7 +352,7 @@
 
 
 def wanted_tables(wanted_ref, block_ref, lane_ref):
-    wanted = wanted_ref[:, 0, :].astype(F32).T[0:CAP].astype(I32)
+    wanted = wanted_ref[:, :, 0, :].reshape(DEVICES, 128).astype(F32).T[0:CAP].astype(I32)
     block_ref[...] = wanted >> 7
     lane_ref[...] = wanted & 127
 
@@ -564,8 +612,8 @@
     rendered_ref, back_ref, back_ninth_ref, owner_row_ref, owner_col_ref, store_sem,
     here_requests_ref, here_params_ref, here_count_ref, here_place_ref, here_slots_ref,
     here_target_ref, load_sem,
-    request_ref, wanted_ref, wanted_block_ref, wanted_lane_ref, request_send, request_receive,
-    request_own,
+    request_ref, middle_ref, wanted_ref, wanted_block_ref, wanted_lane_ref,
+    near_send, near_receive, near_own, far_send, far_receive, far_own,
     screen_ref, ninth_ref, out_ref, out_ninth_ref, split_ref, left_ref, right_ref,
     all_ref, slot_left_ref, slot_right_ref, block_ref, lane_ref, row_ref, col_ref, lanes_ref,
     message_ref, landing_ref, send_sem, receive_sem, own_sem, source_ref, source_ninth_ref,
@@ -593,18 +641,22 @@
     wide = jnp.concatenate(
         [here_requests_ref[...].astype(F32), jnp.zeros((128 - CAP, DEVICES), F32)], axis=0
     )
-    request_ref[:, 0, :] = wide.T.astype(I32)
+    by_device = wide.T.astype(I32).reshape(OUTER, INNER, 128)
+    for inner in range(INNER):
+        request_ref[inner, :, 0, :] = by_device[:, inner, :]
     await_greetings()
-    request_sems = (request_send, request_receive, request_own, me)
-    send_all(request_ref, wanted_ref, *request_sems)
+    near_sems = (near_send, near_receive, near_own)
+    far_sems = (far_send, far_receive, far_own)
+    send_requests(request_ref, middle_ref, near_sems, me)
     for load in loads[1:]:
         load.wait()
     project_all(here_params_ref, screen_ref, ninth_ref)
+    forward_requests(request_ref, middle_ref, wanted_ref, near_sems, far_sems, me)
     index_tables(
         here_count_ref, here_place_ref, here_slots_ref,
         block_ref, lane_ref, row_ref, col_ref, lanes_ref, all_ref, slot_left_ref, slot_right_ref,
     )
-    await_all(request_ref, wanted_ref, *request_sems)
+    await_requests(middle_ref, wanted_ref, far_sems, me)
     wanted_tables(wanted_ref, wanted_block_ref, wanted_lane_ref)
     gather(
         screen_ref, ninth_ref, wanted_block_ref, wanted_lane_ref, out_ref, out_ninth_ref,
@@ -722,7 +774,6 @@
 SPLIT = (3 * (CAP // 2 * 8 + 24), 256)
 SPLIT_BACK = (3 * (SEG // 2 * 8 + 24), 256)
 MESSAGE = (DEVICES, 3, 128)
-REQUEST = (DEVICES, 1, 128)
 TABLE = (CAP, 128)
 STEPS = (SEG_PAD, 128)
 EIGHT = (CAP, 8, 128)
@@ -746,7 +797,8 @@
             vmem((CAP, DEVICES), I32), vmem((PARAMS, OWNED), F32),
             pltpu.SMEM((TILES,), I32), pltpu.SMEM((TILES,), I32), vmem((TILES, SLOTS), I32),
             vmem(IMAGE, F32), pltpu.SemaphoreType.DMA((6,)),
-            vmem(REQUEST, I32), vmem(REQUEST, I32), vmem(TABLE, I32), vmem(TABLE, I32), *sems,
+            vmem((INNER, OUTER, 1, 128), I32), vmem((INNER, OUTER, 1, 128), I32),
+            vmem((OUTER, INNER, 1, 128), I32), vmem(TABLE, I32), vmem(TABLE, I32), *sems, *sems,
             vmem(EIGHT, F32), vmem(NINE, F32), vmem(EIGHT, F32), vmem(TABLE, F32),
             vmem(SPLIT, BF16),
             vmem((2 * BLOCKS, CAP * 128), BF16), vmem((128, CAP * 128), BF16),

time: 53.1 us -> 52 us (0.979)
  Pallas kernels: 52.3 us -> 51.3 us
    pallas_call x1, Pallas kernels: 48.4 us -> 47.3 us  [local(): call(step_kernel, [shape(IMAGE), shape(EIGHT), shape(NINE), shape(TABLE,...]
where the time goes in v4:
time: 52 us; the launch traced here: 51.9 us
  Pallas kernels  51.3 us (99%)
  between operations  0.64 us (1%)
    pallas_call x1, Pallas kernels, local(): call(step_kernel, [shape(IMAGE), shape(EIGHT), shape(NINE), shape(TABLE,...  47.3 us
    pallas_call x1, Pallas kernels, local(): call(pullback_kernel, [shape(IMAGE), shape((PARAMS, OWNED))], 'hhhhhh', '...  3.92 us

profile of v4, /device:TPU:1, one launch (start us, length us, event | category | flops | bytes accessed | tf_op | source)
XLA Modules:
  0.0 51.9 jit_solution(484041343664529102)
XLA Ops:
  0.6 47.3 %step.1 = (f32[3,16,256]{2,1,0:T(8,128)}, f32[40,8,128]{2,1,0:T(8,128)}, f32[5,8,128]{2,1,0:T(8,128)}, s32[40,128]{1,0:T(8,128)}, s32[40,128]{1,0:T(8,128)}) custom-call(s32[40,128]{1,0:T(8,128)} %bitcast.6, f32[59,5120]{1,0:T(8,128)} %params_ref.3, s32[16]{0:T(128)} %count_ref.1, s32[16]{0:T(128)} %place_ref.1, s32[16,512]{1,0:T(8,128)} %slots_ref.1, ...), custom_call_target="tpu_custom_call" | custom-call | tf_op jit(solution)/shard_map/step/pallas_call | solution.py:789
  48.0 3.9 %pullback.1 = (f32[3,16,256]{2,1,0:T(8,128)}, f32[59,5120]{1,0:T(8,128)}) custom-call(f32[40,8,128]{2,1,0:T(8,128)} %get-tuple-element.9.far_source_ref, f32[5,8,128]{2,1,0:T(8,128)} %get-tuple-element.10.far_ninth_ref, s32[40,128]{1,0:T(8,128)} %get-tuple-element.11.far_row_ref, s32[40,128]{1,0:T(8,128)} %get-tuple-element.12.far_col_ref, ...), custom_call_target="tpu_custom_call" | custom-call | tf_op jit(solution)/shard_map/pullback/pallas_call | solution.py:825

commit v5 on v4

--- a/solution.py
+++ b/solution.py
@@ -45,8 +45,9 @@
 SEGS = 12
 GROUP = 8
 PASSES = 32 // GROUP
+MIDDLE = 4
 STEP_UNROLL = 23
-BACK_UNROLL = 2
+BACK_UNROLL = 23
 SHORT_UNROLL = 23
 BF16 = jnp.bfloat16
 MESH_ID = pl.DeviceIdType.MESH
@@ -327,9 +328,24 @@
     pltpu.make_async_copy(wanted_ref.at[others], wanted_ref.at[others], send_sem).wait()
 
 
+def far_first():
+    offsets = [
+        (y, x, z, core) for y in range(4) for x in range(4) for z in range(4) for core in range(2)
+    ]
+    hops = (0, 1, 2, 1)
+    offsets.sort(key=lambda o: -(2 * (hops[o[0]] + hops[o[1]] + hops[o[2]]) + o[3]))
+    return offsets[:-1]
+
+
 def send_all(source_ref, landing_ref, send_sem, receive_sem, own_sem, me):
-    def one(turn, carry):
-        peer = lax.rem(me + turn, DEVICES)
+    at_y, at_x = lax.div(me, 32), lax.rem(lax.div(me, 8), 4)
+    at_z, at_core = lax.rem(lax.div(me, 2), 4), lax.rem(me, 2)
+    to_y = [32 * lax.rem(at_y + turn, 4) for turn in range(4)]
+    to_x = [8 * lax.rem(at_x + turn, 4) for turn in range(4)]
+    to_z = [2 * lax.rem(at_z + turn, 4) for turn in range(4)]
+    to_core = [lax.rem(at_core + turn, 2) for turn in range(2)]
+    for y, x, z, core in far_first():
+        peer = to_y[y] + to_x[x] + to_z[z] + to_core[core]
         pltpu.make_async_remote_copy(
             src_ref=source_ref.at[peer],
             dst_ref=landing_ref.at[me],
@@ -338,9 +354,6 @@
             device_id=(peer,),
             device_id_type=MESH_ID,
         ).start()
-        return carry
-
-    lax.fori_loop(1, DEVICES, one, 0)
     pltpu.make_async_copy(source_ref.at[me], landing_ref.at[me], own_sem).start()
 
 
@@ -458,37 +471,50 @@
 
     repeat(SEG, SHORT_UNROLL, prepare, 0)
 
+    def place(index):
+        half, block = index % 2, index // 2
+        rows = [pl.ds((2 * (GROUP * block + k) + half) * 8, 8) for k in range(GROUP)]
+        return half, GROUP * block + MIDDLE + 0.5, rows
+
     for index in range(PASSES):
-        first_v = index * (GROUP // 2) + 0.5
+        half, middle, rows = place(index)
 
         def one_step(step, state):
             trans, red, green, blue = (list(part) for part in state)
-            opacity, screen_y, curve_y = pre_ref[step, 6], pre_ref[step, 4], pre_ref[step, 5]
+            opacity, curve_y = pre_ref[step, 6], pre_ref[step, 5]
             colours = (pre_ref[step, 7], pre_ref[step, 8], pre_ref[step, 11])
-            for pair in range(GROUP // 2):
-                delta_y = (first_v + float(pair)) - screen_y
-                bend = curve_y * delta_y * delta_y
-                for half in range(2):
-                    k = 2 * pair + half
-                    power = pre_ref[step, half] + (bend + pre_ref[step, 2 + half] * delta_y)
-                    alpha = opacity * jnp.exp2(power)
-                    weight = alpha * trans[k]
-                    trans[k] = trans[k] - weight
-                    red[k] = red[k] + colours[0] * weight
-                    green[k] = green[k] + colours[1] * weight
-                    blue[k] = blue[k] + colours[2] * weight
-                    alpha_ref[index, step, k] = alpha
-                    weight_ref[index, step, k] = weight
+            delta_y = middle - pre_ref[step, 4]
+            bend = curve_y * delta_y
+            slant = pre_ref[step, 2 + half] + bend
+            twice = curve_y + curve_y
+            powers = [None] * GROUP
+            powers[MIDDLE] = pre_ref[step, half] + slant * delta_y
+            slant = slant + bend
+            rise, fall = curve_y + slant, curve_y - slant
+            for k in range(MIDDLE + 1, GROUP):
+                powers[k] = powers[k - 1] + rise
+                rise = rise + twice
+            for k in range(MIDDLE - 1, -1, -1):
+                powers[k] = powers[k + 1] + fall
+                fall = fall + twice
+            for k in range(GROUP):
+                alpha = opacity * jnp.exp2(powers[k])
+                weight = alpha * trans[k]
+                trans[k] = trans[k] - weight
+                red[k] = red[k] + colours[0] * weight
+                green[k] = green[k] + colours[1] * weight
+                blue[k] = blue[k] + colours[2] * weight
+                alpha_ref[index, step, k] = alpha
+                weight_ref[index, step, k] = weight
             return tuple(trans), tuple(red), tuple(green), tuple(blue)
 
         ones = tuple(jnp.ones((8, 128), F32) for _ in range(GROUP))
         zeros = tuple(jnp.zeros((8, 128), F32) for _ in range(GROUP))
         state = repeat(SEG, STEP_UNROLL, one_step, (ones, zeros, zeros, zeros))
         for k in range(GROUP):
-            rows = pl.ds((index * GROUP + k) * 8, 8)
-            trans_ref[rows, :] = state[0][k]
+            trans_ref[rows[k], :] = state[0][k]
             for channel in range(3):
-                colour_ref[channel, rows, :] = state[1 + channel][k]
+                colour_ref[channel, rows[k], :] = state[1 + channel][k]
 
     through = trans_ref[...]
     start = jnp.where(segment == 0, 1.0, pltpu.roll(through, 1, 1))
@@ -519,42 +545,53 @@
     behind_ref[...] = behind * start
 
     for index in range(PASSES):
-        first_v = index * (GROUP // 2) + 0.5
-        rows = [pl.ds((index * GROUP + k) * 8, 8) for k in range(GROUP)]
+        half, middle, rows = place(index)
         errors = [[colour_ref[channel, rows[k], :] for channel in range(3)] for k in range(GROUP)]
 
         def one_step(count, state):
             step = SEG - 1 - count
             state = list(state)
-            screen_y = pre_ref[step, 4]
             colours = (pre_ref[step, 7], pre_ref[step, 8], pre_ref[step, 11])
-            sums = [moment_ref[step, row] if index else None for row in range(9)]
-
-            def add(row, value):
-                sums[row] = value if sums[row] is None else sums[row] + value
-
-            for pair in range(GROUP // 2):
-                delta_y = (first_v + float(pair)) - screen_y
-                for half in range(2):
-                    k = 2 * pair + half
-                    alpha = alpha_ref[index, step, k]
-                    weight = weight_ref[index, step, k]
-                    shade = (
-                        colours[0] * errors[k][0]
-                        + colours[1] * errors[k][1]
-                        + colours[2] * errors[k][2]
-                    )
-                    gap = shade - state[k]
-                    state[k] = state[k] + alpha * gap
-                    slope = weight * gap
-                    slope_y = slope * delta_y
-                    add(3 * half, slope)
-                    add(3 * half + 1, slope_y)
-                    add(3 * half + 2, slope_y * delta_y)
-                    for channel in range(3):
-                        add(6 + channel, weight * errors[k][channel])
-            for row in range(9):
-                moment_ref[step, row] = sums[row]
+            slopes = [None] * GROUP
+            shares = [None, None, None]
+            for k in range(GROUP):
+                alpha = alpha_ref[index, step, k]
+                weight = weight_ref[index, step, k]
+                shade = (
+                    colours[0] * errors[k][0]
+                    + colours[1] * errors[k][1]
+                    + colours[2] * errors[k][2]
+                )
+                gap = shade - state[k]
+                state[k] = state[k] + alpha * gap
+                slopes[k] = weight * gap
+                for channel in range(3):
+                    part = weight * errors[k][channel]
+                    shares[channel] = part if k == 0 else shares[channel] + part
+            flat = tilt = bend = None
+            for order in (range(GROUP - 1, MIDDLE, -1), range(MIDDLE)):
+                first = second = third = None
+                for k in order:
+                    first = slopes[k] if first is None else first + slopes[k]
+                    second = first if second is None else second + first
+                    third = second if third is None else third + second
+                square = (third + third) - second
+                flat = first if flat is None else flat + first
+                bend = square if bend is None else bend + square
+                tilt = second if tilt is None else tilt - second
+            flat = flat + slopes[MIDDLE]
+            delta_y = middle - pre_ref[step, 4]
+            moved = tilt + delta_y * flat
+            bend = bend + delta_y * (tilt + moved)
+            for row, value, started in (
+                (3 * half, flat, index > 1),
+                (3 * half + 1, moved, index > 1),
+                (3 * half + 2, bend, index > 1),
+                (6, shares[0], index > 0),
+                (7, shares[1], index > 0),
+                (8, shares[2], index > 0),
+            ):
+                moment_ref[step, row] = moment_ref[step, row] + value if started else value
             return tuple(state)
 
         repeat(

time: 52 us -> 49 us (0.942)
  Pallas kernels: 51.3 us -> 48.2 us
    pallas_call x1, Pallas kernels: 47.3 us -> 44.3 us  [local(): call(step_kernel, [shape(IMAGE), shape(EIGHT), shape(NINE), shape(TABLE,...]
where the time goes in v5:
time: 49 us; the launch traced here: 48.8 us
  Pallas kernels  48.2 us (98%)
  between operations  0.64 us (1%)
    pallas_call x1, Pallas kernels, local(): call(step_kernel, [shape(IMAGE), shape(EIGHT), shape(NINE), shape(TABLE,...  44.3 us
    pallas_call x1, Pallas kernels, local(): call(pullback_kernel, [shape(IMAGE), shape((PARAMS, OWNED))], 'hhhhhh', '...  3.92 us

profile of v5, /device:TPU:1, one launch (start us, length us, event | category | flops | bytes accessed | tf_op | source)
XLA Modules:
  0.0 48.8 jit_solution(9254119491188733477)
XLA Ops:
  0.6 44.3 %step.1 = (f32[3,16,256]{2,1,0:T(8,128)}, f32[40,8,128]{2,1,0:T(8,128)}, f32[5,8,128]{2,1,0:T(8,128)}, s32[40,128]{1,0:T(8,128)}, s32[40,128]{1,0:T(8,128)}) custom-call(s32[40,128]{1,0:T(8,128)} %bitcast.6, f32[59,5120]{1,0:T(8,128)} %params_ref.3, s32[16]{0:T(128)} %count_ref.1, s32[16]{0:T(128)} %place_ref.1, s32[16,512]{1,0:T(8,128)} %slots_ref.1, ...), custom_call_target="tpu_custom_call" | custom-call | tf_op jit(solution)/shard_map/step/pallas_call | solution.py:826
  44.9 3.9 %pullback.1 = (f32[3,16,256]{2,1,0:T(8,128)}, f32[59,5120]{1,0:T(8,128)}) custom-call(f32[40,8,128]{2,1,0:T(8,128)} %get-tuple-element.9.far_source_ref, f32[5,8,128]{2,1,0:T(8,128)} %get-tuple-element.10.far_ninth_ref, s32[40,128]{1,0:T(8,128)} %get-tuple-element.11.far_row_ref, s32[40,128]{1,0:T(8,128)} %get-tuple-element.12.far_col_ref, ...), custom_call_target="tpu_custom_call" | custom-call | tf_op jit(solution)/shard_map/pullback/pallas_call | solution.py:862

commit v6 on v5

--- a/solution.py
+++ b/solution.py
@@ -143,7 +143,7 @@
 
 def gather(
     source_ref, ninth_ref, block_ref, lane_ref, out_ref, out_ninth_ref, split_ref,
-    targets, sources, by_matmul, by_lanes,
+    targets, sources, by_matmul, by_lanes, parts=3,
 ):
     half = sources // 2
     eights = half * 8
@@ -164,7 +164,7 @@
         ],
         axis=1,
     )
-    for part in range(3):
+    for part in range(parts):
         for values, start in ((main, 0), (rest, eights)):
             rounded = values.astype(BF16)
             split_ref[part * height + start : part * height + start + values.shape[0]] = rounded
@@ -184,8 +184,8 @@
         place = block - half * upper
         match = jnp.concatenate([key] * 16, axis=0) == iota
         pick = jnp.where(match, jnp.ones((), BF16), jnp.zeros((), BF16))
-        parts = lax.dot_general(
-            split_ref[...], pick, (((1,), (0,)), ((), ())), preferred_element_type=F32
+        products = lax.dot_general(
+            split_ref[0 : parts * height], pick, (((1,), (0,)), ((), ())), preferred_element_type=F32
         )
         for k in range(by_lanes):
             row = base + by_matmul + k
@@ -206,7 +206,9 @@
                 )
                 total = jnp.where(offset == 8 * source, picked, total)
             out_ninth_ref[pl.ds(row, 1), :] = jnp.sum(total, axis=0, keepdims=True)
-        values = (parts[0:height] + parts[height : 2 * height]) + parts[2 * height : 3 * height]
+        values = products[0:height]
+        for part in range(1, parts):
+            values = values + products[part * height : (part + 1) * height]
         wide = jnp.broadcast_to(place, (8, width))
         total = jnp.zeros((8, width), F32)
         for source in range(half):
@@ -521,20 +523,26 @@
     for shift in (1, 2, 4, 8):
         start = start * jnp.where(segment >= shift, pltpu.roll(start, shift, 1), 1.0)
     pick = jnp.where(lax.broadcasted_iota(I32, (TILES, 128), 0) == tile, 1.0, 0.0)
+    colours = [colour_ref[channel] for channel in range(3)]
+    images = lax.dot_general(
+        pick, jnp.concatenate([colour * start for colour in colours], axis=0),
+        (((1,), (1,)), ((), ())),
+        preferred_element_type=F32, precision=lax.Precision.HIGHEST,
+    )
+    errors = []
+    for channel in range(3):
+        image = images[:, 256 * channel : 256 * channel + 256]
+        rendered_ref[channel] = image
+        errors.append((image - target_ref[channel]) * (1.0 / 256.0))
+    spread = lax.dot_general(
+        jnp.concatenate(errors, axis=1), pick, (((0,), (0,)), ((), ())),
+        preferred_element_type=F32, precision=lax.Precision.HIGHEST,
+    )
     behind = jnp.zeros((256, 128), F32)
     for channel in range(3):
-        image = lax.dot_general(
-            pick, colour_ref[channel] * start, (((1,), (1,)), ((), ())),
-            preferred_element_type=F32, precision=lax.Precision.HIGHEST,
-        )
-        rendered_ref[channel] = image
-        error = (image - target_ref[channel]) * (1.0 / 256.0)
-        spread = lax.dot_general(
-            error, pick, (((0,), (0,)), ((), ())),
-            preferred_element_type=F32, precision=lax.Precision.HIGHEST,
-        )
-        behind = behind + spread * colour_ref[channel]
-        colour_ref[channel] = spread * start
+        part = spread[256 * channel : 256 * channel + 256]
+        behind = behind + part * colours[channel]
+        colour_ref[channel] = part * start
     left = segments - 1 - segment
     factor = jnp.where(left >= 1, pltpu.roll(through, 127, 1), 0.0)
     behind = jnp.where(left >= 1, pltpu.roll(behind, 127, 1), 0.0)
@@ -638,15 +646,15 @@
     grad_ninth_ref[...] = ninth_ref[...].reshape(SEG_PAD // 8, 8, 128)
     gather(
         grad_ref, grad_ninth_ref, row_ref, col_ref, back_ref, back_ninth_ref, split_back_ref,
-        CAP, SEG, 10, 10,
+        CAP, SEG, 10, 10, 2,
     )
     pack_messages(back_ref, back_ninth_ref, gradient_ref)
 
 
 def step_kernel(
     requests_ref, params_ref, count_ref, place_ref, slots_ref, target_ref,
-    far_rendered_ref, far_back_ref, far_back_ninth_ref, far_owner_row_ref, far_owner_col_ref,
-    rendered_ref, back_ref, back_ninth_ref, owner_row_ref, owner_col_ref, store_sem,
+    far_rendered_ref, reply_landing_ref, far_owner_row_ref, far_owner_col_ref,
+    rendered_ref, owner_row_ref, owner_col_ref, store_sem,
     here_requests_ref, here_params_ref, here_count_ref, here_place_ref, here_slots_ref,
     here_target_ref, load_sem,
     request_ref, middle_ref, wanted_ref, wanted_block_ref, wanted_lane_ref,
@@ -654,7 +662,7 @@
     screen_ref, ninth_ref, out_ref, out_ninth_ref, split_ref, left_ref, right_ref,
     all_ref, slot_left_ref, slot_right_ref, block_ref, lane_ref, row_ref, col_ref, lanes_ref,
     message_ref, landing_ref, send_sem, receive_sem, own_sem, source_ref, source_ninth_ref,
-    reply_ref, reply_landing_ref, reply_send, reply_receive, reply_own,
+    reply_ref, reply_send, reply_receive, reply_own,
     *render_refs,
 ):
     me = lax.axis_index("dev")
@@ -721,33 +729,27 @@
                 (rendered_ref, far_rendered_ref),
                 (owner_row_ref, far_owner_row_ref),
                 (owner_col_ref, far_owner_col_ref),
-                (back_ref, far_back_ref),
-                (back_ninth_ref, far_back_ninth_ref),
             )
         )
     ]
-    for store in stores[:3]:
+    for store in stores:
         store.start()
     await_all(reply_ref, reply_landing_ref, *reply_sems)
-    unpack_messages(reply_landing_ref, back_ref, back_ninth_ref)
-    for store in stores[3:]:
-        store.start()
     for store in stores:
         store.wait()
 
 
 def pullback_kernel(
-    far_source_ref, far_ninth_ref, far_row_ref, far_col_ref, image_ref, params_ref,
+    far_message_ref, far_row_ref, far_col_ref, image_ref, params_ref,
     rendered_ref, gradient_ref,
-    source_ref, source_ninth_ref, row_ref, col_ref,
+    message_ref, source_ref, source_ninth_ref, row_ref, col_ref,
     rows_ref, ninth_ref, split_ref, here_params_ref, here_gradient_ref, load_sem, store_sem,
 ):
     loads = [
         pltpu.make_async_copy(far, near, load_sem.at[index])
         for index, (far, near) in enumerate(
             (
-                (far_source_ref, source_ref),
-                (far_ninth_ref, source_ninth_ref),
+                (far_message_ref, message_ref),
                 (far_row_ref, row_ref),
                 (far_col_ref, col_ref),
                 (params_ref, here_params_ref),
@@ -757,13 +759,14 @@
     ]
     for load in loads:
         load.start()
-    for load in loads[:4]:
+    for load in loads[:3]:
         load.wait()
+    unpack_messages(message_ref, source_ref, source_ninth_ref)
     gather(
         source_ref, source_ninth_ref, row_ref, col_ref, rows_ref, ninth_ref, split_ref,
-        BLOCKS, CAP, 10, 10,
-    )
-    loads[4].wait()
+        BLOCKS, CAP, 10, 10, 2,
+    )
+    loads[3].wait()
     stores = []
     for group in range(OWNED // 1024):
         columns = pl.ds(group * 1024, 1024)
@@ -785,7 +788,7 @@
         stores[-1].start()
     for store in stores:
         store.wait()
-    loads[5].wait()
+    loads[4].wait()
 
 
 def shape(dims, dtype=F32):
@@ -823,14 +826,13 @@
 def local(params, requests, tile_slots, tile_count, tile_place, target):
     vmem = pltpu.VMEM
     sems = [pltpu.SemaphoreType.DMA] * 3
-    image, back, back_ninth, owner_row, owner_col = call(
+    image, replies, owner_row, owner_col = call(
         step_kernel,
-        [shape(IMAGE), shape(EIGHT), shape(NINE), shape(TABLE, I32), shape(TABLE, I32)],
+        [shape(IMAGE), shape(MESSAGE), shape(TABLE, I32), shape(TABLE, I32)],
         "hhhhhh",
-        "hhhhh",
+        "hhhh",
         [
-            vmem(IMAGE, F32), vmem(EIGHT, F32), vmem(NINE, F32), vmem(TABLE, I32),
-            vmem(TABLE, I32), pltpu.SemaphoreType.DMA((5,)),
+            vmem(IMAGE, F32), vmem(TABLE, I32), vmem(TABLE, I32), pltpu.SemaphoreType.DMA((3,)),
             vmem((CAP, DEVICES), I32), vmem((PARAMS, OWNED), F32),
             pltpu.SMEM((TILES,), I32), pltpu.SMEM((TILES,), I32), vmem((TILES, SLOTS), I32),
             vmem(IMAGE, F32), pltpu.SemaphoreType.DMA((6,)),
@@ -844,7 +846,7 @@
             vmem(STEPS, I32), vmem(STEPS, I32), vmem(TABLE, I32), vmem(TABLE, I32),
             vmem((8, 128), I32),
             vmem(MESSAGE, F32), vmem(MESSAGE, F32), *sems, vmem(EIGHT, F32), vmem(NINE, F32),
-            vmem(MESSAGE, F32), vmem(MESSAGE, F32), *sems,
+            vmem(MESSAGE, F32), *sems,
             vmem((SEG, 8, 128), F32), vmem(STEPS, F32),
             vmem((SEG, 12, 8, 128), F32),
             vmem((PASSES, SEG, GROUP, 8, 128), F32), vmem((PASSES, SEG, GROUP, 8, 128), F32),
@@ -862,16 +864,16 @@
     rendered, gradient = call(
         pullback_kernel,
         [shape(IMAGE), shape((PARAMS, OWNED))],
-        "hhhhhh",
+        "hhhhh",
         "hh",
         [
-            vmem(EIGHT, F32), vmem(NINE, F32), vmem(TABLE, I32), vmem(TABLE, I32),
+            vmem(MESSAGE, F32), vmem(EIGHT, F32), vmem(NINE, F32), vmem(TABLE, I32), vmem(TABLE, I32),
             vmem(EIGHT, F32), vmem(TABLE, F32), vmem(SPLIT, BF16), vmem((PARAMS, OWNED), F32),
-            vmem((PARAMS, OWNED), F32), pltpu.SemaphoreType.DMA((6,)),
+            vmem((PARAMS, OWNED), F32), pltpu.SemaphoreType.DMA((5,)),
             pltpu.SemaphoreType.DMA((OWNED // 1024,)),
         ],
         "pullback",
-    )(back, back_ninth, owner_row, owner_col, image, params)
+    )(replies, owner_row, owner_col, image, params)
     return rendered.transpose(1, 0, 2), gradient
 
 

time: 49 us -> 47.6 us (0.971)
  Pallas kernels: 48.2 us -> 46.8 us
    pallas_call x2, Pallas kernels: 48.2 us -> 46.8 us  [the longest x1 42.8 us: local(): call(step_kernel, [shape(IMAGE), shape(MESSAGE), shape(TABLE, I32), shape...]
where the time goes in v6:
time: 47.6 us; the launch traced here: 47.5 us
  Pallas kernels  46.8 us (98%)
  between operations  0.64 us (1%)
    pallas_call x1, Pallas kernels, local(): call(step_kernel, [shape(IMAGE), shape(MESSAGE), shape(TABLE, I32), shape...  42.8 us
    pallas_call x1, Pallas kernels, local(): call(pullback_kernel, [shape(IMAGE), shape((PARAMS, OWNED))], 'hhhhh', 'h...  4.03 us

profile of v6, /device:TPU:1, one launch (start us, length us, event | category | flops | bytes accessed | tf_op | source)
XLA Modules:
  0.0 47.5 jit_solution(14749354122296148978)
XLA Ops:
  0.6 42.8 %step.1 = (f32[3,16,256]{2,1,0:T(8,128)}, f32[128,3,128]{2,1,0:T(4,128)}, s32[40,128]{1,0:T(8,128)}, s32[40,128]{1,0:T(8,128)}) custom-call(s32[40,128]{1,0:T(8,128)} %bitcast.6, f32[59,5120]{1,0:T(8,128)} %params_ref.3, s32[16]{0:T(128)} %count_ref.1, s32[16]{0:T(128)} %place_ref.1, s32[16,512]{1,0:T(8,128)} %slots_ref.1, f32[3,16,256]{2,1,0:T(8,128)} %bitcast.5), custom_call_target="tpu_custom_call" | custom-call | tf_op jit(solution)/shard_map/step/pallas_call | solution.py:829
  43.4 4.0 %pullback.1 = (f32[3,16,256]{2,1,0:T(8,128)}, f32[59,5120]{1,0:T(8,128)}) custom-call(f32[128,3,128]{2,1,0:T(4,128)} %get-tuple-element.8.far_message_ref, s32[40,128]{1,0:T(8,128)} %get-tuple-element.9.far_row_ref, s32[40,128]{1,0:T(8,128)} %get-tuple-element.10.far_col_ref, f32[3,16,256]{2,1,0:T(8,128)} %get-tuple-element.11.image_ref, f32[59,5120]{1,0:T(8,128)} %params_ref.3), custom_call_target="tpu_custom_call" | custom-call | tf_op jit(solution)/shard_map/pullback/pallas_call | solution.py:864

commit v7 on v6

--- a/solution.py
+++ b/solution.py
@@ -646,7 +646,7 @@
     grad_ninth_ref[...] = ninth_ref[...].reshape(SEG_PAD // 8, 8, 128)
     gather(
         grad_ref, grad_ninth_ref, row_ref, col_ref, back_ref, back_ninth_ref, split_back_ref,
-        CAP, SEG, 10, 10, 2,
+        CAP, SEG, 14, 6, 2,
     )
     pack_messages(back_ref, back_ninth_ref, gradient_ref)
 
@@ -764,7 +764,7 @@
     unpack_messages(message_ref, source_ref, source_ninth_ref)
     gather(
         source_ref, source_ninth_ref, row_ref, col_ref, rows_ref, ninth_ref, split_ref,
-        BLOCKS, CAP, 10, 10, 2,
+        BLOCKS, CAP, 12, 8, 2,
     )
     loads[3].wait()
     stores = []

time: 47.6 us -> 47.1 us (0.989)
  no operation moved by 1% of the time
where the time goes in v7:
time: 47.1 us; the launch traced here: 47 us
  Pallas kernels  46.4 us (99%)
  between operations  0.64 us (1%)
    pallas_call x1, Pallas kernels, local(): call(step_kernel, [shape(IMAGE), shape(MESSAGE), shape(TABLE, I32), shape...  42.5 us
    pallas_call x1, Pallas kernels, local(): call(pullback_kernel, [shape(IMAGE), shape((PARAMS, OWNED))], 'hhhhh', 'h...  3.85 us

profile of v7, /device:TPU:1, one launch (start us, length us, event | category | flops | bytes accessed | tf_op | source)
XLA Modules:
  0.0 47.0 jit_solution(17020909535333009497)
XLA Ops:
  0.6 42.5 %step.1 = (f32[3,16,256]{2,1,0:T(8,128)}, f32[128,3,128]{2,1,0:T(4,128)}, s32[40,128]{1,0:T(8,128)}, s32[40,128]{1,0:T(8,128)}) custom-call(s32[40,128]{1,0:T(8,128)} %bitcast.6, f32[59,5120]{1,0:T(8,128)} %params_ref.3, s32[16]{0:T(128)} %count_ref.1, s32[16]{0:T(128)} %place_ref.1, s32[16,512]{1,0:T(8,128)} %slots_ref.1, f32[3,16,256]{2,1,0:T(8,128)} %bitcast.5), custom_call_target="tpu_custom_call" | custom-call | tf_op jit(solution)/shard_map/step/pallas_call | solution.py:829
  43.1 3.9 %pullback.1 = (f32[3,16,256]{2,1,0:T(8,128)}, f32[59,5120]{1,0:T(8,128)}) custom-call(f32[128,3,128]{2,1,0:T(4,128)} %get-tuple-element.8.far_message_ref, s32[40,128]{1,0:T(8,128)} %get-tuple-element.9.far_row_ref, s32[40,128]{1,0:T(8,128)} %get-tuple-element.10.far_col_ref, f32[3,16,256]{2,1,0:T(8,128)} %get-tuple-element.11.image_ref, f32[59,5120]{1,0:T(8,128)} %params_ref.3), custom_call_target="tpu_custom_call" | custom-call | tf_op jit(solution)/shard_map/pullback/pallas_call | solution.py:864
